TPU v7x, 256 devices: a whole 4x4x8 slice. The times are simulated.
256 devices in a mesh: row: 16 (over z, x_lo), col: 16 (over x_hi, y, core).
Axes of the slice: x: 4 (x_hi: 2, x_lo: 2; x = x_hi * 2 + x_lo), y: 4, z: 8, core: 2. Of those that a mesh axis runs over, the one named last changes fastest.
Arguments:
- patches: bfloat16 [512, 256, 768], P('row', 'col'), may hold values from -6 to 6
- norm_gain: float32 [768], replicated, may hold values from 0.25 to 1.75
- w_qkv: bfloat16 [768, 2304], replicated, may hold values from -0.21875 to 0.21875
- pool_q: float32 [9, 768], replicated, may hold values from -30 to 30, as said below
- pool_kv: float32 [9, 1536], replicated, may hold values from -2 to 2
- w_out: bfloat16 [768, 768], replicated, may hold values from -0.21875 to 0.21875
Outputs:
- mixed: bfloat16 [256, 128, 768], P('row', 'col')
Inputs may be any that keep to these rules, and one draw needn't show every extreme that they name: `pool_q`: query pooling taps, nonzero, of either sign.
All inputs are finite; a program needn't handle non-finite values.
Results may differ from a plain program's by a relative error of at most 0.017.
The roundings to bfloat16 on the way count: a program that leaves them out, or rounds other values in their place, can miss the bound.
Values may be sent and summed in bfloat16 or wider, within the bound.
No kernel may reach another device: no remote copies, remote signals or barrier semaphores. Data moves between devices by JAX's collectives and lax.ppermute only.
A program may use at most 128 MiB of HBM per device.

v0:
```python
import functools
import math

import jax
import jax.numpy as jnp
from jax import lax
from jax.experimental import pallas as pl
from jax.experimental.pallas import tpu as pltpu
from jax.sharding import Mesh
from jax.sharding import PartitionSpec as P

AXES = ("za", "zl", "xl", "xh", "y", "core")
ROW = ("za", "zl", "xl")
COL = ("xh", "y", "core")
HEAD = 64
GROUP = 3
WIDE = GROUP * HEAD
SCALE = HEAD**-0.5 * math.log2(math.e)
STATS = 16
bf16, f32 = jnp.bfloat16, jnp.float32


def shifted(block, axis, distance):
    count = lax.axis_size(axis)
    return lax.ppermute(block, axis, [(i, (i + distance) % count) for i in range(count)])


def shifted_x(block, distance):
    place = lambda i: (i % 2) * 2 + i // 2
    route = [(place(i), place((i + distance) % 4)) for i in range(4)]
    return lax.ppermute(block, ("xl", "xh"), route)


def passed_along(block, axis):
    count = lax.axis_size(axis)
    return lax.ppermute(block, axis, [(i - 1, i) for i in range(1, count)])


def corner(block):
    rows, cols = lax.axis_size(ROW), lax.axis_size(COL)
    route = [((r - 1) * cols + c - 1, r * cols + c) for r in range(1, rows) for c in range(1, cols)]
    return lax.ppermute(block, AXES, route)


def normalised(values, gain):
    center = values - jnp.mean(values, axis=-1, keepdims=True)
    spread = jnp.mean(center * center, axis=-1, keepdims=True)
    return (center * lax.rsqrt(spread + 1e-06) * gain).astype(bf16)


def project(tokens, weights):
    return jnp.dot(tokens, weights, preferred_element_type=f32).astype(bf16)


ORDER = (0, 1, 3, 4, 5, 7, 8, 9, 11, 12, 13, 2, 6, 10, 14, 15)
KEY_COLUMNS = 11


def keep(plain, values):
    for k in range(plain.shape[0]):
        plain[k] = values[:, 128 * k : 128 * (k + 1)]


def every_nth(plain, start, step):
    picked = [plain[k, pl.ds(start, 8, stride=step), :] for k in range(plain.shape[0])]
    return jnp.concatenate(picked, 1)


def own_kernel(patches_ref, gain_ref, wq_ref, wk_ref, wv_ref, q_ref, kv_ref, plain, tokens):
    rows, cols, width = patches_ref.shape
    keep(plain, patches_ref[...].astype(f32).reshape(rows * cols, width))
    gain = gain_ref[...]
    for place, c in enumerate(ORDER):
        parts = [every_nth(plain, 16 * r + c, 64) for r in range(4)]
        tokens[pl.ds(32 * place, 32), :] = normalised(jnp.concatenate(parts, 0), gain)
    few = tokens[: 32 * KEY_COLUMNS]
    kv_ref[:, :width] = project(few, wk_ref[...])
    kv_ref[:, width:] = project(few, wv_ref[...])
    q_ref[...] = project(tokens[...], wq_ref[...])


def column_of_w(i):
    return pl.BlockSpec((768, 768), lambda _: (0, i))


def whole(shape):
    return pl.BlockSpec(shape, lambda _: (0,) * len(shape))


def project_own(patches, gain, w_qkv):
    rows, cols, width = patches.shape
    count = rows * cols
    shapes = [(count, width), (32 * KEY_COLUMNS, 2 * width)]
    return pl.pallas_call(
        own_kernel,
        grid=(1,),
        in_specs=[whole(patches.shape), whole(gain.shape)] + [column_of_w(i) for i in range(3)],
        out_specs=[whole(s) for s in shapes],
        out_shape=[jax.ShapeDtypeStruct(s, bf16) for s in shapes],
        scratch_shapes=[pltpu.VMEM((width // 128, count, 128), f32), pltpu.VMEM((count, width), bf16)],
        compiler_params=pltpu.CompilerParams(vmem_limit_bytes=48 * 2**20),
        cost_estimate=pl.CostEstimate(flops=1_400_000_000, bytes_accessed=6_000_000, transcendentals=0),
    )(patches, gain, w_qkv, w_qkv, w_qkv)


def halo_tokens(upper_ref, left_ref, corner_ref, gain_ref, plain):
    keep(plain, left_ref[...].astype(f32))
    left = jnp.concatenate([every_nth(plain, r, 4) for r in range(4)], 0)
    rest = jnp.zeros((15, left.shape[1]), f32)
    every = [left, upper_ref[...].astype(f32), corner_ref[...].astype(f32), rest]
    return normalised(jnp.concatenate(every, 0), gain_ref[...])


def columns_of(own_ref, halo, columns):
    first = lax.broadcasted_iota(jnp.int32, (8, own_ref.shape[1]), 0) == 0
    groups = {}
    for c in columns:
        if c < 0:
            block, above = halo[0:32], halo[48:49]
        else:
            place = ORDER.index(c)
            block, above = own_ref[pl.ds(32 * place, 32), :].astype(f32), halo[32 + c : 33 + c]
        four = [block[8 * r : 8 * r + 8] for r in range(4)]
        groups[c] = [jnp.where(first, above, pltpu.roll(four[3], 1, 0))] + four
    return groups


def pooled(groups, taps, column, row):
    total = None
    for a in range(3):
        for b in range(3):
            term = taps[3 * a + b] * groups[column + b - 1][row + a]
            total = term if total is None else total + term
    return total


def keyvals_kernel(own_ref, upper_ref, left_ref, corner_ref, gain_ref, wk_ref, wv_ref, pool_ref, out_ref, plain):
    tokens = halo_tokens(upper_ref, left_ref, corner_ref, gain_ref, plain)
    width = wk_ref.shape[1]
    both = []
    for part, w_ref in enumerate((wk_ref, wv_ref)):
        cols = pl.ds(part * width, width)
        halo = project(tokens, w_ref[...]).astype(f32)
        taps = [pool_ref[t : t + 1, cols] for t in range(9)]
        groups = columns_of(own_ref.at[:, cols], halo, (-1,) + ORDER[:KEY_COLUMNS])
        both.append(jnp.concatenate([pooled(groups, taps, 4 * j, 0) for j in range(4)], 0))
    for g in range(out_ref.shape[0]):
        lanes = slice(g * WIDE, (g + 1) * WIDE)
        out_ref[g] = jnp.concatenate([p[:, lanes] for p in both], 1).astype(bf16)


def queries_kernel(own_ref, upper_ref, left_ref, corner_ref, gain_ref, w_ref, pool_ref, out_ref, plain):
    tokens = halo_tokens(upper_ref, left_ref, corner_ref, gain_ref, plain)
    halo = project(tokens, w_ref[...]).astype(f32)
    taps = [pool_ref[t : t + 1, :] for t in range(9)]
    groups = columns_of(own_ref, halo, range(-1, 16))
    rows = [pooled(groups, taps, 2 * j, 2 * p) for j in range(8) for p in range(2)]
    turned = jnp.concatenate(rows, 0).T.astype(bf16)
    count = out_ref.shape[0] // 2
    for g in range(count):
        block = turned[g * WIDE : (g + 1) * WIDE]
        out_ref[g] = block
        out_ref[count + g] = block


def pool_call(kernel, own, halo, gain, w_qkv, parts, taps, out_shape):
    return pl.pallas_call(
        kernel,
        grid=(1,),
        in_specs=[whole(a.shape) for a in (own, *halo, gain)]
        + [column_of_w(i) for i in parts]
        + [whole(taps.shape)],
        out_specs=whole(out_shape),
        out_shape=jax.ShapeDtypeStruct(out_shape, bf16),
        scratch_shapes=[pltpu.VMEM((gain.shape[1] // 128, 32, 128), f32)],
        compiler_params=pltpu.CompilerParams(vmem_limit_bytes=48 * 2**20),
        cost_estimate=pl.CostEstimate(flops=200_000_000, bytes_accessed=4_000_000, transcendentals=0),
    )(own, *halo, gain, *([w_qkv] * len(parts)), taps)


def attend_kernel(first, last, block, qb, q_ref, kv_ref, *refs):
    if first:
        carry_in = None
    else:
        carry_in, refs = refs[:2], refs[2:]
    outs, (qz, stat, acc) = refs[:-3], refs[-3:]
    step = pl.program_id(0)
    tiles = q_ref.shape[0]
    count = tiles * 128

    @pl.when(step == 0)
    def _():
        zero = jnp.zeros((HEAD, count), bf16)
        q = jnp.concatenate([q_ref[t] for t in range(tiles)], axis=1)
        qz[0] = jnp.concatenate([q[:HEAD], zero], 0)
        qz[1] = jnp.concatenate([zero, q[HEAD : 2 * HEAD]], 0)
        qz[2] = jnp.concatenate([q[2 * HEAD :], zero], 0)
        if first:
            stat[0:8] = jnp.full((8, count), -1e30, f32)
            stat[8:16] = jnp.zeros((8, count), f32)
            acc[...] = jnp.zeros_like(acc)
        else:
            stat[...] = carry_in[0][...]
            acc[...] = carry_in[1][...]

    values = kv_ref[:, 128:384].T
    ones = jnp.ones((16, block), bf16)
    jobs = [(h, j) for j in range(count // qb) for h in range(GROUP)]

    def scores(h, j):
        keys = kv_ref[:, 0:128] if h < 2 else kv_ref[:, 128:256]
        return jnp.dot(keys, qz[h, :, j * qb : (j + 1) * qb], preferred_element_type=f32)

    ready = scores(*jobs[0])
    for place, (h, j) in enumerate(jobs):
        now = ready
        if place + 1 < len(jobs):
            ready = scores(*jobs[place + 1])
        lanes = slice(j * qb, (j + 1) * qb)
        old = stat[h : h + 1, lanes]
        new = jnp.maximum(old, jnp.max(now, axis=0, keepdims=True))
        factor = jnp.exp2((old - new) * SCALE)
        weights = jnp.exp2((now - new) * SCALE).astype(bf16)
        stat[h : h + 1, lanes] = new
        value = jnp.concatenate([values[HEAD * (h + 1) : HEAD * (h + 2)], ones], 0)
        part = jnp.dot(value, weights, preferred_element_type=f32)
        rows = slice(HEAD * h, HEAD * (h + 1))
        stat[8 + h : 9 + h, lanes] = stat[8 + h : 9 + h, lanes] * factor + part[HEAD : HEAD + 1]
        acc[rows, lanes] = acc[rows, lanes] * factor + part[:HEAD]

    @pl.when(step == pl.num_programs(0) - 1)
    def _():
        if not last:
            outs[0][...] = stat[...]
            outs[1][...] = acc[...]
            return
        total = stat[8:16]
        logs = stat[0:8] * SCALE + jnp.log2(jnp.maximum(total, 1e-30))
        high = logs.astype(bf16)
        left = logs - high.astype(f32)
        middle = left.astype(bf16)
        low = (left - middle.astype(f32)).astype(bf16)
        three = [a.astype(f32)[:GROUP] for a in (high, middle, low)]
        packed = jnp.concatenate(three + [jnp.zeros((STATS - 9, count), f32)], 0).astype(bf16)
        for t in range(tiles):
            lanes = slice(t * 128, (t + 1) * 128)
            for h in range(GROUP):
                rows = slice(HEAD * h, HEAD * (h + 1))
                outs[0][t, rows] = (acc[rows, lanes] / total[h : h + 1, lanes]).astype(bf16)
            outs[0][t, WIDE:] = packed[:, lanes]


def attend(queries, keyvals, carry, last, block=512, qb=512):
    tiles = queries.shape[0]
    count = tiles * 128
    keys = keyvals.shape[0]
    block = min(block, keys)
    carry_shapes = [(16, count), (WIDE, count)]
    carry_specs = [whole(s) for s in carry_shapes]
    if last:
        out_shape = jax.ShapeDtypeStruct((tiles, WIDE + STATS, 128), bf16)
        out_specs = whole(out_shape.shape)
    else:
        out_shape = [jax.ShapeDtypeStruct(s, f32) for s in carry_shapes]
        out_specs = carry_specs
    work = GROUP * count * keys
    return pl.pallas_call(
        functools.partial(attend_kernel, carry is None, last, block, qb),
        grid=(keys // block,),
        in_specs=[whole(queries.shape), pl.BlockSpec((block, 2 * WIDE), lambda i: (i, 0))]
        + ([] if carry is None else carry_specs),
        out_specs=out_specs,
        out_shape=out_shape,
        scratch_shapes=[
            pltpu.VMEM((GROUP, 128, count), bf16),
            pltpu.VMEM((16, count), f32),
            pltpu.VMEM((WIDE, count), f32),
        ],
        compiler_params=pltpu.CompilerParams(vmem_limit_bytes=48 * 2**20),
        cost_estimate=pl.CostEstimate(
            flops=work * 1024, bytes_accessed=keys * 768, transcendentals=work
        ),
    )(queries, keyvals, *(carry or ()))


def finish_kernel(parts_ref, w_ref, out_ref, rows):
    groups = parts_ref.shape[0] // 2
    pieces = []
    for g in range(groups):
        pair = [parts_ref[g], parts_ref[groups + g]]
        logs = []
        for p in pair:
            s = p[WIDE:].astype(f32)
            logs.append((s[0:3] + s[3:6]) + s[6:9])
        top = jnp.maximum(logs[0], logs[1])
        shares = [jnp.exp2(a - top) for a in logs]
        total = shares[0] + shares[1]
        for h in range(GROUP):
            head = slice(HEAD * h, HEAD * (h + 1))
            both = [p[head].astype(f32) * (s[h : h + 1] / total[h : h + 1]) for p, s in zip(pair, shares)]
            pieces.append(both[0] + both[1])
    attended = jnp.concatenate(pieces, 0).T.astype(bf16)
    keep(rows, jnp.dot(attended, w_ref[...], preferred_element_type=f32))
    for r in range(out_ref.shape[0]):
        start = 8 * (r % 2) + r // 2
        out_ref[r] = every_nth(rows, start, 16).astype(bf16)


def finish(parts, w_out):
    shape = (parts.shape[2], w_out.shape[1])
    return pl.pallas_call(
        finish_kernel,
        out_shape=jax.ShapeDtypeStruct((16, 8, shape[1]), bf16),
        scratch_shapes=[pltpu.VMEM((shape[1] // 128, shape[0], 128), f32)],
        compiler_params=pltpu.CompilerParams(vmem_limit_bytes=48 * 2**20),
    )(parts, w_out)


def on_device(patches, norm_gain, w_qkv, pool_q, pool_kv, w_out):
    upper = passed_along(patches[-1:], ROW)
    left = passed_along(patches[:, -1:], COL)
    above_left = corner(patches[-1:, -1:])
    gain = norm_gain[None]
    own_q, own_kv = project_own(patches, gain, w_qkv)
    halo = (upper[0], left[:, 0], above_left[0])
    groups = lax.axis_size("zl")
    flat = pool_call(keyvals_kernel, own_kv, halo, gain, w_qkv, (1, 2), pool_kv, (groups, 32, 2 * WIDE))
    own = lax.all_to_all(flat, "zl", 0, 0, tiled=True).reshape(-1, 2 * WIDE)
    turned = pool_call(queries_kernel, own_q, halo, gain, w_qkv, (0,), pool_q, (2 * groups, WIDE, 128))
    every_query = lax.all_to_all(turned, ("za", "zl"), 0, 0, tiled=True)
    line = jnp.concatenate([own, shifted_x(own, 1), shifted_x(own, -1), shifted_x(own, 2)], 0)
    swap = lambda block: shifted(block, "core", 1)
    after, before = shifted(line, "y", 1), shifted(line, "y", -1)
    half = line.shape[0] // 2
    far = [shifted(after[:half], "y", 1), shifted(before[half:], "y", -1)]
    carry = attend(every_query, line, None, False)
    carry = attend(every_query, swap(line), carry, False)
    for block in (after, swap(after), before, swap(before)):
        carry = attend(every_query, block, carry, False)
    far = jnp.concatenate(far, 0)
    carry = attend(every_query, far, carry, False)
    partial = attend(every_query, swap(far), carry, True)
    parts = lax.all_to_all(partial, ("za", "zl"), 0, 0, tiled=True)
    return finish(parts, w_out)


def solution(mesh):
    fine = Mesh(mesh.devices.reshape(2, 4, 2, 2, 4, 2), AXES)
    tiles = P(ROW, COL, None)
    return jax.shard_map(
        on_device,
        mesh=fine,
        in_specs=(tiles, P(), P(), P(), P(), P()),
        out_specs=tiles,
        check_vma=False,
    )
```

profile of v0, /device:TPU:1, one launch (start us, length us, event | category | flops | bytes accessed | tf_op | source)
XLA Modules:
  0.0 109.7 jit_solution(5455627437679014099)
XLA Ops:
  0.0 1.1 %slice.16 = bf16[32,1,768]{2,1,0:T(2,128)(2,1)S(1)} slice(bf16[32,16,768]{2,1,0:T(8,128)(2,1)} %patches_ref.1), slice={[0:32], [15:16], [0:768]} | slice | bytes 98304 | tf_op jit(solution)/shard_map/slice | solution.py:321
  1.1 4.6 %collective-permute-start.1 = (bf16[32,1,768]{2,0,1:T(8,128)(2,1)S(1)}, bf16[32,1,768]{2,0,1:T(8,128)(2,1)S(1)}, u32[]{:S(2)}, u32[]{:S(2)}) collective-permute-start(bf16[32,1,768]{2,0,1:T(8,128)(2,1)S(1)} %copy.8), channel_id=1, source_target_pairs={{0,1},{1,2},{2,3},{3,4},{4,5},{5,6},{6,7},{7,8},{8,9},{9,10},{10,1... | collective-permute-start | bytes 147464 | tf_op jit(solution)/shard_map/ppermute | solution.py:36
  6.5 3.1 %collective-permute-start = (bf16[1,16,768]{2,1,0:T(8,128)(2,1)S(1)}, bf16[1,16,768]{2,1,0:T(8,128)(2,1)S(1)}, u32[]{:S(2)}, u32[]{:S(2)}) collective-permute-start(bf16[1,16,768]{2,1,0:T(8,128)(2,1)S(1)} %slice.15), channel_id=1, source_target_pairs={{0,16},{16,32},{32,48},{48,64},{64,80},{80,96},{96,112},{112,128},... | collective-permute-start | bytes 73736 | tf_op jit(solution)/shard_map/ppermute | solution.py:36
  10.3 3.5 %collective-permute-start.2 = (bf16[1,1,768]{2,1,0:T(2,128)(2,1)S(1)}, bf16[1,1,768]{2,1,0:T(2,128)(2,1)S(1)}, u32[]{:S(2)}, u32[]{:S(2)}) collective-permute-start(bf16[1,1,768]{2,1,0:T(2,128)(2,1)S(1)} %slice.17), channel_id=1, source_target_pairs={{0,17},{1,18},{2,19},{3,20},{4,21},{5,22},{6,23},{7,24},{8,25},{9,... | collective-permute-start | bytes 4616 | tf_op jit(solution)/shard_map/ppermute | solution.py:42
  14.5 2.0 %copy-done = bf16[768,2304]{1,0:T(8,128)(2,1)S(1)} copy-done((bf16[768,2304]{1,0:T(8,128)(2,1)S(1)}, bf16[768,2304]{1,0:T(8,128)(2,1)}, u32[]{:S(2)}) %copy-start) | copy-done | bytes 3538968
  16.5 1.1 %copy-done.4 = bf16[32,16,768]{2,1,0:T(8,128)(2,1)S(1)} copy-done((bf16[32,16,768]{2,1,0:T(8,128)(2,1)S(1)}, bf16[32,16,768]{2,1,0:T(8,128)(2,1)}, u32[]{:S(2)}) %copy-start.4) | copy-done | bytes 786456
  17.6 3.1 %shard_map.64 = (bf16[512,768]{1,0:T(8,128)(2,1)S(1)}, bf16[352,1536]{1,0:T(8,128)(2,1)S(1)}) custom-call(bf16[32,16,768]{2,1,0:T(8,128)(2,1)S(1)} %copy-done.4, f32[1,768]{1,0:T(1,128)S(1)} %broadcast_in_dim.3.gain_ref, bf16[768,2304]{1,0:T(8,128)(2,1)S(1)} %copy-done, bf16[768,2304]{1,0:T(8,128)(2,1)S(1)} %copy-done, bf16[768,2304]{1,0:T(8,128)(2,1)S(1)} %copy-done), custom_call_target="tpu_custom_call" | custom-call | flops 1400000000 | bytes 6000000 | tf_op jit(solution)/shard_map/pallas_call | solution.py:94
  24.3 6.8 %all-to-all-start.1 = ((bf16[4,32,384]{2,1,0:T(8,128)(2,1)}), bf16[4,32,384]{2,1,0:T(8,128)(2,1)}, u32[]{:S(2)}, u32[]{:S(2)}) async-start(bf16[4,32,384]{2,1,0:T(8,128)(2,1)} %copy-done.7), calls=%async_computation.1 | async-start | bytes 196608 | tf_op jit(solution)/shard_map/all_to_all | solution.py:328
  31.2 1.1 %copy-done.6 = bf16[512,768]{1,0:T(8,128)(2,1)S(1)} copy-done((bf16[512,768]{1,0:T(8,128)(2,1)S(1)}, bf16[512,768]{1,0:T(8,128)(2,1)}, u32[]{:S(2)}) %copy-start.6) | copy-done | bytes 786456
  36.2 4.6 %all-to-all-start = ((bf16[8,192,128]{2,1,0:T(8,128)(2,1)}), bf16[8,192,128]{2,1,0:T(8,128)(2,1)S(1)}, u32[]{:S(2)}, u32[]{:S(2)}) async-start(bf16[8,192,128]{2,1,0:T(8,128)(2,1)} %copy-done.2), calls=%async_computation | async-start | bytes 786432 | tf_op jit(solution)/shard_map/all_to_all | solution.py:330
  40.8 1.2 %collective-permute-start.3 = (bf16[128,384]{1,0:T(8,128)(2,1)}, bf16[128,384]{1,0:T(8,128)(2,1)S(1)}, u32[]{:S(2)}, u32[]{:S(2)}) collective-permute-start(bf16[128,384]{1,0:T(8,128)(2,1)} %bitcast.3), channel_id=1, source_target_pairs={{0,16},{16,8},{8,24},{24,0},{1,17},{17,9},{9,25},{25,1},{2,18},{18... | collective-permute-start | bytes 294920 | tf_op jit(solution)/shard_map/ppermute | solution.py:31
  42.0 1.5 %collective-permute-start.4 = (bf16[128,384]{1,0:T(8,128)(2,1)}, bf16[128,384]{1,0:T(8,128)(2,1)S(1)}, u32[]{:S(2)}, u32[]{:S(2)}) collective-permute-start(bf16[128,384]{1,0:T(8,128)(2,1)} %bitcast.3), channel_id=1, source_target_pairs={{0,24},{16,0},{8,16},{24,8},{1,25},{17,1},{9,17},{25,9},{2,26},{18... | collective-permute-start | bytes 294920 | tf_op jit(solution)/shard_map/ppermute | solution.py:31
  43.5 1.5 %collective-permute-start.5 = (bf16[128,384]{1,0:T(8,128)(2,1)}, bf16[128,384]{1,0:T(8,128)(2,1)S(1)}, u32[]{:S(2)}, u32[]{:S(2)}) collective-permute-start(bf16[128,384]{1,0:T(8,128)(2,1)} %bitcast.3), channel_id=1, source_target_pairs={{0,8},{16,24},{8,0},{24,16},{1,9},{17,25},{9,1},{25,17},{2,10},{18... | collective-permute-start | bytes 294920 | tf_op jit(solution)/shard_map/ppermute | solution.py:31
  45.7 4.3 %collective-permute-done.5 = bf16[128,384]{1,0:T(8,128)(2,1)S(1)} collective-permute-done((bf16[128,384]{1,0:T(8,128)(2,1)}, bf16[128,384]{1,0:T(8,128)(2,1)S(1)}, u32[]{:S(2)}, u32[]{:S(2)}) %collective-permute-start.5) | collective-permute-done | bytes 98336 | tf_op jit(solution)/shard_map/ppermute | solution.py:31
  49.9 0.9 pad_maximum_fusion.kv_ref
  50.9 1.4 %collective-permute-start.6 = (bf16[512,384]{1,0:T(8,128)(2,1)S(1)}, bf16[512,384]{1,0:T(8,128)(2,1)S(1)}, u32[]{:S(2)}, u32[]{:S(2)}) collective-permute-start(bf16[512,384]{1,0:T(8,128)(2,1)S(1)} %pad_maximum_fusion.kv_ref), channel_id=1, source_target_pairs={{0,2},{2,4},{4,6},{6,0},{1,3},{3,5},{5,7},{7,1},{8,10},{10,12},{12... | collective-permute-start | bytes 1179656 | tf_op jit(solution)/shard_map/ppermute | solution.py:25
  52.2 1.4 %collective-permute-start.8 = (bf16[512,384]{1,0:T(8,128)(2,1)S(1)}, bf16[512,384]{1,0:T(8,128)(2,1)S(1)}, u32[]{:S(2)}, u32[]{:S(2)}) collective-permute-start(bf16[512,384]{1,0:T(8,128)(2,1)S(1)} %pad_maximum_fusion.kv_ref), channel_id=1, source_target_pairs={{0,6},{2,0},{4,2},{6,4},{1,7},{3,1},{5,3},{7,5},{8,14},{10,8},{12,... | collective-permute-start | bytes 1179656 | tf_op jit(solution)/shard_map/ppermute | solution.py:25
  53.6 3.3 %collective-permute-start.13 = (bf16[512,384]{1,0:T(8,128)(2,1)S(1)}, bf16[512,384]{1,0:T(8,128)(2,1)S(1)}, u32[]{:S(2)}, u32[]{:S(2)}) collective-permute-start(bf16[512,384]{1,0:T(8,128)(2,1)S(1)} %pad_maximum_fusion.kv_ref), channel_id=1, source_target_pairs={{0,1},{1,0},{2,3},{3,2},{4,5},{5,4},{6,7},{7,6},{8,9},{9,8},{10,11... | collective-permute-start | bytes 1179656 | tf_op jit(solution)/shard_map/ppermute | solution.py:25
  56.9 3.2 %collective-permute-done.6.kv_ref = bf16[512,384]{1,0:T(8,128)(2,1)S(1)} collective-permute-done((bf16[512,384]{1,0:T(8,128)(2,1)S(1)}, bf16[512,384]{1,0:T(8,128)(2,1)S(1)}, u32[]{:S(2)}, u32[]{:S(2)}) %collective-permute-start.6) | collective-permute-done | bytes 393248 | tf_op jit(solution)/shard_map/ppermute | solution.py:25
  60.2 0.9 collective-permute-start.7
  61.1 1.9 %collective-permute-start.9 = (bf16[256,384]{1,0:T(8,128)(2,1)S(1)}, bf16[256,384]{1,0:T(8,128)(2,1)S(1)}, u32[]{:S(2)}, u32[]{:S(2)}) collective-permute-start(bf16[256,384]{1,0:T(8,128)(2,1)S(1)} %slice.21), channel_id=1, source_target_pairs={{0,6},{2,0},{4,2},{6,4},{1,7},{3,1},{5,3},{7,5},{8,14},{10,8},{12,... | collective-permute-start | bytes 589832 | tf_op jit(solution)/shard_map/ppermute | solution.py:25
  63.0 4.1 %collective-permute-start.12 = (bf16[512,384]{1,0:T(8,128)(2,1)S(1)}, bf16[512,384]{1,0:T(8,128)(2,1)S(1)}, u32[]{:S(2)}, u32[]{:S(2)}) collective-permute-start(bf16[512,384]{1,0:T(8,128)(2,1)S(1)} %collective-permute-done.6.kv_ref), channel_id=1, source_target_pairs={{0,1},{1,0},{2,3},{3,2},{4,5},{5,4},{6,7},{7,6},{8,9},{9,8},{10,11... | collective-permute-start | bytes 1179656 | tf_op jit(solution)/shard_map/ppermute | solution.py:25
  67.2 2.3 %shard_map.67 = (f32[16,1024]{1,0:T(8,128)S(1)}, f32[192,1024]{1,0:T(8,128)S(1)}) custom-call(bf16[8,192,128]{2,1,0:T(8,128)(2,1)S(1)} %all-to-all-done.q_ref, bf16[512,384]{1,0:T(8,128)(2,1)S(1)} %pad_maximum_fusion.kv_ref), custom_call_target="tpu_custom_call" | custom-call | flops 1610612736 | bytes 393216 | tf_op jit(solution)/shard_map/pallas_call | solution.py:267
  69.4 2.3 %shard_map.68 = (f32[16,1024]{1,0:T(8,128)S(1)}, f32[192,1024]{1,0:T(8,128)S(1)}) custom-call(bf16[8,192,128]{2,1,0:T(8,128)(2,1)S(1)} %all-to-all-done.q_ref, bf16[512,384]{1,0:T(8,128)(2,1)S(1)} %collective-permute-done.13.kv_ref, f32[16,1024]{1,0:T(8,128)S(1)} %get-tuple-element.23.refs_0_, f32[192,1024]{1,0:T(8,128)S(1)} %get-tuple-element.24.refs_1_), custom_call_target="tpu_custom_call" | custom-call | flops 1610612736 | bytes 393216 | tf_op jit(solution)/shard_map/pallas_call | solution.py:267
  71.7 2.3 %shard_map.69 = (f32[16,1024]{1,0:T(8,128)S(1)}, f32[192,1024]{1,0:T(8,128)S(1)}) custom-call(bf16[8,192,128]{2,1,0:T(8,128)(2,1)S(1)} %all-to-all-done.q_ref, bf16[512,384]{1,0:T(8,128)(2,1)S(1)} %collective-permute-done.6.kv_ref, f32[16,1024]{1,0:T(8,128)S(1)} %get-tuple-element.25.refs_0_, f32[192,1024]{1,0:T(8,128)S(1)} %get-tuple-element.26.refs_1_), custom_call_target="tpu_custom_call" | custom-call | flops 1610612736 | bytes 393216 | tf_op jit(solution)/shard_map/pallas_call | solution.py:267
  74.7 2.3 %shard_map.70 = (f32[16,1024]{1,0:T(8,128)S(1)}, f32[192,1024]{1,0:T(8,128)S(1)}) custom-call(bf16[8,192,128]{2,1,0:T(8,128)(2,1)S(1)} %all-to-all-done.q_ref, bf16[512,384]{1,0:T(8,128)(2,1)S(1)} %collective-permute-done.12.kv_ref, f32[16,1024]{1,0:T(8,128)S(1)} %get-tuple-element.27.refs_0_, f32[192,1024]{1,0:T(8,128)S(1)} %get-tuple-element.28.refs_1_), custom_call_target="tpu_custom_call" | custom-call | flops 1610612736 | bytes 393216 | tf_op jit(solution)/shard_map/pallas_call | solution.py:267
  77.1 2.3 %shard_map.71 = (f32[16,1024]{1,0:T(8,128)S(1)}, f32[192,1024]{1,0:T(8,128)S(1)}) custom-call(bf16[8,192,128]{2,1,0:T(8,128)(2,1)S(1)} %all-to-all-done.q_ref, bf16[512,384]{1,0:T(8,128)(2,1)S(1)} %collective-permute-done.8.kv_ref, f32[16,1024]{1,0:T(8,128)S(1)} %get-tuple-element.29.refs_0_, f32[192,1024]{1,0:T(8,128)S(1)} %get-tuple-element.30.refs_1_), custom_call_target="tpu_custom_call" | custom-call | flops 1610612736 | bytes 393216 | tf_op jit(solution)/shard_map/pallas_call | solution.py:267
  79.4 2.3 %shard_map.72 = (f32[16,1024]{1,0:T(8,128)S(1)}, f32[192,1024]{1,0:T(8,128)S(1)}) custom-call(bf16[8,192,128]{2,1,0:T(8,128)(2,1)S(1)} %all-to-all-done.q_ref, bf16[512,384]{1,0:T(8,128)(2,1)S(1)} %collective-permute-done.11.kv_ref, f32[16,1024]{1,0:T(8,128)S(1)} %get-tuple-element.31.refs_0_, f32[192,1024]{1,0:T(8,128)S(1)} %get-tuple-element.32.refs_1_), custom_call_target="tpu_custom_call" | custom-call | flops 1610612736 | bytes 393216 | tf_op jit(solution)/shard_map/pallas_call | solution.py:267
  81.7 2.3 %shard_map.73 = (f32[16,1024]{1,0:T(8,128)S(1)}, f32[192,1024]{1,0:T(8,128)S(1)}) custom-call(bf16[8,192,128]{2,1,0:T(8,128)(2,1)S(1)} %all-to-all-done.q_ref, bf16[512,384]{1,0:T(8,128)(2,1)S(1)} %constant_dynamic-update-slice_fusion.kv_ref, f32[16,1024]{1,0:T(8,128)S(1)} %get-tuple-element.33.refs_0_, f32[192,1024]{1,0:T(8,128)S(1)} %get-tuple-element.34.refs_1_), custom_call_target="tpu_custom_call" | custom-call | flops 1610612736 | bytes 393216 | tf_op jit(solution)/shard_map/pallas_call | solution.py:267
  84.0 2.3 %shard_map.74 = bf16[8,208,128]{2,1,0:T(8,128)(2,1)S(1)} custom-call(bf16[8,192,128]{2,1,0:T(8,128)(2,1)S(1)} %all-to-all-done.q_ref, bf16[512,384]{1,0:T(8,128)(2,1)S(1)} %collective-permute-done.10.kv_ref, f32[16,1024]{1,0:T(8,128)S(1)} %get-tuple-element.35.refs_0_, f32[192,1024]{1,0:T(8,128)S(1)} %get-tuple-element.36.refs_1_), custom_call_target="tpu_custom_call" | custom-call | flops 1610612736 | bytes 393216 | tf_op jit(solution)/shard_map/pallas_call | solution.py:267
  86.4 22.2 %all_to_all.15.parts_ref = bf16[8,208,128]{2,1,0:T(8,128)(2,1)S(1)} all-to-all(bf16[8,208,128]{2,1,0:T(8,128)(2,1)S(1)} %shard_map.74), channel_id=1, replica_groups=mesh['za'=2,'zl'=4,'xl'=2,'xh'=2,'y'=4,'core'=2] {'za','zl'}, dimensions={0} | all-to-all | bytes 851968 | tf_op jit(solution)/shard_map/all_to_all | solution.py:343
  108.6 1.1 %shard_map.75 = bf16[16,8,768]{2,1,0:T(8,128)(2,1)} custom-call(bf16[8,208,128]{2,1,0:T(8,128)(2,1)S(1)} %all_to_all.15.parts_ref, bf16[768,768]{1,0:T(8,128)(2,1)S(1)} %copy-done.3), custom_call_target="tpu_custom_call" | custom-call | tf_op jit(solution)/shard_map/pallas_call | solution.py:311
  (51 shorter events, 11.0 us)
Async XLA Ops:
  1.1 20.5 %collective-permute-start.1 = (bf16[32,1,768]{2,0,1:T(8,128)(2,1)S(1)}, bf16[32,1,768]{2,0,1:T(8,128)(2,1)S(1)}, u32[]{:S(2)}, u32[]{:S(2)}) collective-permute-start(bf16[32,1,768]{2,0,1:T(8,128)(2,1)S(1)} %copy.8), channel_id=1, source_target_pairs={{0,1},{1,2},{2,3},{3,4},{4,5},{5,6},{6,7},{7,8},{8,9},{9,10},{10,1... | collective-permute-start | bytes 147464 | tf_op jit(solution)/shard_map/ppermute | solution.py:36
  6.5 15.1 %collective-permute-start = (bf16[1,16,768]{2,1,0:T(8,128)(2,1)S(1)}, bf16[1,16,768]{2,1,0:T(8,128)(2,1)S(1)}, u32[]{:S(2)}, u32[]{:S(2)}) collective-permute-start(bf16[1,16,768]{2,1,0:T(8,128)(2,1)S(1)} %slice.15), channel_id=1, source_target_pairs={{0,16},{16,32},{32,48},{48,64},{64,80},{80,96},{96,112},{112,128},... | collective-permute-start | bytes 73736 | tf_op jit(solution)/shard_map/ppermute | solution.py:36
  10.3 11.3 %collective-permute-start.2 = (bf16[1,1,768]{2,1,0:T(2,128)(2,1)S(1)}, bf16[1,1,768]{2,1,0:T(2,128)(2,1)S(1)}, u32[]{:S(2)}, u32[]{:S(2)}) collective-permute-start(bf16[1,1,768]{2,1,0:T(2,128)(2,1)S(1)} %slice.17), channel_id=1, source_target_pairs={{0,17},{1,18},{2,19},{3,20},{4,21},{5,22},{6,23},{7,24},{8,25},{9,... | collective-permute-start | bytes 4616 | tf_op jit(solution)/shard_map/ppermute | solution.py:42
  14.5 2.0 %copy-start = (bf16[768,2304]{1,0:T(8,128)(2,1)S(1)}, bf16[768,2304]{1,0:T(8,128)(2,1)}, u32[]{:S(2)}) copy-start(bf16[768,2304]{1,0:T(8,128)(2,1)} %wv_ref.3) | copy-start | bytes 10616836
  16.5 1.1 %copy-start.4 = (bf16[32,16,768]{2,1,0:T(8,128)(2,1)S(1)}, bf16[32,16,768]{2,1,0:T(8,128)(2,1)}, u32[]{:S(2)}) copy-start(bf16[32,16,768]{2,1,0:T(8,128)(2,1)} %patches_ref.1) | copy-start | bytes 2359300
  17.6 4.0 %copy-start.1 = (bf16[768,2304]{1,0:T(8,128)(2,1)S(1)}, bf16[768,2304]{1,0:T(8,128)(2,1)}, u32[]{:S(2)}) copy-start(bf16[768,2304]{1,0:T(8,128)(2,1)} %wv_ref.3) | copy-start | bytes 10616836
  17.6 4.0 %copy-start.10 = (f32[9,1536]{1,0:T(8,128)S(1)}, f32[9,1536]{1,0:T(8,128)}, u32[]{:S(2)}) copy-start(f32[9,1536]{1,0:T(8,128)} %pool_ref.3) | copy-start | bytes 165892
  20.7 0.9 copy-start.5
  22.5 0.6 copy-start.7
  23.1 0.6 copy-start.8
  23.7 0.6 copy-start.11
  24.3 11.8 %all-to-all-start.1 = ((bf16[4,32,384]{2,1,0:T(8,128)(2,1)}), bf16[4,32,384]{2,1,0:T(8,128)(2,1)}, u32[]{:S(2)}, u32[]{:S(2)}) async-start(bf16[4,32,384]{2,1,0:T(8,128)(2,1)} %copy-done.7), calls=%async_computation.1 | async-start | bytes 196608 | tf_op jit(solution)/shard_map/all_to_all | solution.py:328
  31.2 1.1 %copy-start.6 = (bf16[512,768]{1,0:T(8,128)(2,1)S(1)}, bf16[512,768]{1,0:T(8,128)(2,1)}, u32[]{:S(2)}) copy-start(bf16[512,768]{1,0:T(8,128)(2,1)} %copy-done.5) | copy-start | bytes 2359300
  32.3 0.8 copy-start.9
  33.1 0.7 copy-start.12
  33.8 0.8 copy-start.13
  35.4 0.8 copy-start.2
  36.2 31.0 %all-to-all-start = ((bf16[8,192,128]{2,1,0:T(8,128)(2,1)}), bf16[8,192,128]{2,1,0:T(8,128)(2,1)S(1)}, u32[]{:S(2)}, u32[]{:S(2)}) async-start(bf16[8,192,128]{2,1,0:T(8,128)(2,1)} %copy-done.2), calls=%async_computation | async-start | bytes 786432 | tf_op jit(solution)/shard_map/all_to_all | solution.py:330
  40.8 4.9 %collective-permute-start.3 = (bf16[128,384]{1,0:T(8,128)(2,1)}, bf16[128,384]{1,0:T(8,128)(2,1)S(1)}, u32[]{:S(2)}, u32[]{:S(2)}) collective-permute-start(bf16[128,384]{1,0:T(8,128)(2,1)} %bitcast.3), channel_id=1, source_target_pairs={{0,16},{16,8},{8,24},{24,0},{1,17},{17,9},{9,25},{25,1},{2,18},{18... | collective-permute-start | bytes 294920 | tf_op jit(solution)/shard_map/ppermute | solution.py:31
  42.0 3.7 %collective-permute-start.4 = (bf16[128,384]{1,0:T(8,128)(2,1)}, bf16[128,384]{1,0:T(8,128)(2,1)S(1)}, u32[]{:S(2)}, u32[]{:S(2)}) collective-permute-start(bf16[128,384]{1,0:T(8,128)(2,1)} %bitcast.3), channel_id=1, source_target_pairs={{0,24},{16,0},{8,16},{24,8},{1,25},{17,1},{9,17},{25,9},{2,26},{18... | collective-permute-start | bytes 294920 | tf_op jit(solution)/shard_map/ppermute | solution.py:31
  43.5 6.5 %collective-permute-start.5 = (bf16[128,384]{1,0:T(8,128)(2,1)}, bf16[128,384]{1,0:T(8,128)(2,1)S(1)}, u32[]{:S(2)}, u32[]{:S(2)}) collective-permute-start(bf16[128,384]{1,0:T(8,128)(2,1)} %bitcast.3), channel_id=1, source_target_pairs={{0,8},{16,24},{8,0},{24,16},{1,9},{17,25},{9,1},{25,17},{2,10},{18... | collective-permute-start | bytes 294920 | tf_op jit(solution)/shard_map/ppermute | solution.py:31
  50.9 9.3 %collective-permute-start.6 = (bf16[512,384]{1,0:T(8,128)(2,1)S(1)}, bf16[512,384]{1,0:T(8,128)(2,1)S(1)}, u32[]{:S(2)}, u32[]{:S(2)}) collective-permute-start(bf16[512,384]{1,0:T(8,128)(2,1)S(1)} %pad_maximum_fusion.kv_ref), channel_id=1, source_target_pairs={{0,2},{2,4},{4,6},{6,0},{1,3},{3,5},{5,7},{7,1},{8,10},{10,12},{12... | collective-permute-start | bytes 1179656 | tf_op jit(solution)/shard_map/ppermute | solution.py:25
  52.2 8.8 %collective-permute-start.8 = (bf16[512,384]{1,0:T(8,128)(2,1)S(1)}, bf16[512,384]{1,0:T(8,128)(2,1)S(1)}, u32[]{:S(2)}, u32[]{:S(2)}) collective-permute-start(bf16[512,384]{1,0:T(8,128)(2,1)S(1)} %pad_maximum_fusion.kv_ref), channel_id=1, source_target_pairs={{0,6},{2,0},{4,2},{6,4},{1,7},{3,1},{5,3},{7,5},{8,14},{10,8},{12,... | collective-permute-start | bytes 1179656 | tf_op jit(solution)/shard_map/ppermute | solution.py:25
  53.6 15.8 %collective-permute-start.13 = (bf16[512,384]{1,0:T(8,128)(2,1)S(1)}, bf16[512,384]{1,0:T(8,128)(2,1)S(1)}, u32[]{:S(2)}, u32[]{:S(2)}) collective-permute-start(bf16[512,384]{1,0:T(8,128)(2,1)S(1)} %pad_maximum_fusion.kv_ref), channel_id=1, source_target_pairs={{0,1},{1,0},{2,3},{3,2},{4,5},{5,4},{6,7},{7,6},{8,9},{9,8},{10,11... | collective-permute-start | bytes 1179656 | tf_op jit(solution)/shard_map/ppermute | solution.py:25
  60.2 13.9 %collective-permute-start.7 = (bf16[256,384]{1,0:T(8,128)(2,1)S(1)}, bf16[256,384]{1,0:T(8,128)(2,1)S(1)}, u32[]{:S(2)}, u32[]{:S(2)}) collective-permute-start(bf16[256,384]{1,0:T(8,128)(2,1)S(1)} %slice.20), channel_id=1, source_target_pairs={{0,2},{2,4},{4,6},{6,0},{1,3},{3,5},{5,7},{7,1},{8,10},{10,12},{12... | collective-permute-start | bytes 589832 | tf_op jit(solution)/shard_map/ppermute | solution.py:25
  61.1 13.0 %collective-permute-start.9 = (bf16[256,384]{1,0:T(8,128)(2,1)S(1)}, bf16[256,384]{1,0:T(8,128)(2,1)S(1)}, u32[]{:S(2)}, u32[]{:S(2)}) collective-permute-start(bf16[256,384]{1,0:T(8,128)(2,1)S(1)} %slice.21), channel_id=1, source_target_pairs={{0,6},{2,0},{4,2},{6,4},{1,7},{3,1},{5,3},{7,5},{8,14},{10,8},{12,... | collective-permute-start | bytes 589832 | tf_op jit(solution)/shard_map/ppermute | solution.py:25
  63.0 11.7 %collective-permute-start.12 = (bf16[512,384]{1,0:T(8,128)(2,1)S(1)}, bf16[512,384]{1,0:T(8,128)(2,1)S(1)}, u32[]{:S(2)}, u32[]{:S(2)}) collective-permute-start(bf16[512,384]{1,0:T(8,128)(2,1)S(1)} %collective-permute-done.6.kv_ref), channel_id=1, source_target_pairs={{0,1},{1,0},{2,3},{3,2},{4,5},{5,4},{6,7},{7,6},{8,9},{9,8},{10,11... | collective-permute-start | bytes 1179656 | tf_op jit(solution)/shard_map/ppermute | solution.py:25
  67.1 12.2 %collective-permute-start.11 = (bf16[512,384]{1,0:T(8,128)(2,1)S(1)}, bf16[512,384]{1,0:T(8,128)(2,1)S(1)}, u32[]{:S(2)}, u32[]{:S(2)}) collective-permute-start(bf16[512,384]{1,0:T(8,128)(2,1)S(1)} %collective-permute-done.8.kv_ref), channel_id=1, source_target_pairs={{0,1},{1,0},{2,3},{3,2},{4,5},{5,4},{6,7},{7,6},{8,9},{9,8},{10,11... | collective-permute-start | bytes 1179656 | tf_op jit(solution)/shard_map/ppermute | solution.py:25
  74.2 9.9 %collective-permute-start.10 = (bf16[512,384]{1,0:T(8,128)(2,1)S(1)}, bf16[512,384]{1,0:T(8,128)(2,1)S(1)}, u32[]{:S(2)}, u32[]{:S(2)}) collective-permute-start(bf16[512,384]{1,0:T(8,128)(2,1)S(1)} %constant_dynamic-update-slice_fusion.kv_ref), channel_id=1, source_target_pairs={{0,1},{1,0},{2,3},{3,2},{4,5},{5,4},{6,7},{7,6},{8,9},{9,8},{10,11... | collective-permute-start | bytes 1179656 | tf_op jit(solution)/shard_map/ppermute | solution.py:25
  84.0 24.5 %copy-start.3 = (bf16[768,768]{1,0:T(8,128)(2,1)S(1)}, bf16[768,768]{1,0:T(8,128)(2,1)}, u32[]{:S(2)}) copy-start(bf16[768,768]{1,0:T(8,128)(2,1)} %w_ref.3) | copy-start | bytes 3538948
where the time goes:
time: 111 us; the launch traced here: 110 us
  starting transfers between devices  40.4 us (36%)
  Pallas kernels  24.3 us (22%)
  blocking collectives  22.2 us (20%)
  local copies, waits for them, and re-layouts  13.5 us (12%)
  waiting for transfers between devices  8.22 us (7%)
    all_to_all x1, blocking collectives, on_device(): parts = lax.all_to_all(partial, ('za', 'zl'), 0, 0, tiled=True)  22.2 us
    pallas_call x8, Pallas kernels, attend(): pl.pallas_call(functools.partial(attend_kernel, carry is None, last, bloc...  18.5 us
    ppermute x8, starting transfers between devices, shifted(): lax.ppermute(block, axis, [(i, (i + distance) % count) for i in range(cou...  13.6 us
    unnamed x30, local copies, waits for them, and re-layouts  10.1 us
    ppermute x2, starting transfers between devices, passed_along(): return lax.ppermute(block, axis, [(i - 1, i) for i in range(1, count)])  7.7 us
    all_to_all x1, starting transfers between devices, on_device(): own = lax.all_to_all(flat, 'zl', 0, 0, tiled=True).reshape(-1, 2 * WIDE)  6.83 us
    ppermute x3, waiting for transfers between devices, shifted_x(): return lax.ppermute(block, ('xl', 'xh'), route)  4.94 us
    all_to_all x1, starting transfers between devices, on_device(): every_query = lax.all_to_all(turned, ('za', 'zl'), 0, 0, tiled=True)  4.62 us
  transfers between devices with their start and end apart: 16, of which 3 were waited for; matrix products, arithmetic and copies ran while one was open for 3% of the time, Pallas kernels for 18%

commit v1 on v0

--- a/solution.py
+++ b/solution.py
@@ -9,8 +9,8 @@
 from jax.sharding import Mesh
 from jax.sharding import PartitionSpec as P
 
-AXES = ("za", "zl", "xl", "xh", "y", "core")
-ROW = ("za", "zl", "xl")
+AXES = ("zq", "zc", "xl", "xh", "y", "core")
+ROW = ("zq", "zc", "xl")
 COL = ("xh", "y", "core")
 HEAD = 64
 GROUP = 3
@@ -66,17 +66,52 @@
     return jnp.concatenate(picked, 1)
 
 
-def own_kernel(patches_ref, gain_ref, wq_ref, wk_ref, wv_ref, q_ref, kv_ref, plain, tokens):
-    rows, cols, width = patches_ref.shape
-    keep(plain, patches_ref[...].astype(f32).reshape(rows * cols, width))
+def edge_kernel(right_ref, low_ref, column_ref, row_ref, corner_ref, plain):
+    rows, cols, width = right_ref.shape
+    keep(plain, right_ref[...].astype(f32).reshape(rows * cols, width))
+    column = jnp.concatenate([every_nth(plain, 8 * r + cols - 1, 32) for r in range(4)], 0)
+    column_ref[...] = column.astype(bf16)
+    last = low_ref[0]
+    row_ref[...] = last
+    corner_ref[...] = last[-1:]
+
+
+def edges(patches):
+    rows, cols, width = patches.shape
+    shapes = [(rows, width), (cols, width), (1, width)]
+    return pl.pallas_call(
+        edge_kernel,
+        grid=(1,),
+        in_specs=[
+            pl.BlockSpec((rows, 8, width), lambda _: (0, cols // 8 - 1, 0)),
+            pl.BlockSpec((1, cols, width), lambda _: (rows - 1, 0, 0)),
+        ],
+        out_specs=[whole(s) for s in shapes],
+        out_shape=[jax.ShapeDtypeStruct(s, bf16) for s in shapes],
+        scratch_shapes=[pltpu.VMEM((width // 128, 8 * rows, 128), f32)],
+        compiler_params=pltpu.CompilerParams(vmem_limit_bytes=60 * 2**20),
+        cost_estimate=pl.CostEstimate(flops=0, bytes_accessed=1_000_000, transcendentals=0),
+    )(patches, patches)
+
+
+def own_kernel(patches_ref, gain_ref, w_ref, q_ref, kv_ref, patches, weights, plain, tokens, sems):
+    rows, cols, width = patches.shape
+    copies = [
+        pltpu.make_async_copy(patches_ref, patches, sems.at[0]),
+        pltpu.make_async_copy(w_ref, weights, sems.at[1]),
+    ]
+    for copy in copies:
+        copy.start()
+    copies[0].wait()
+    keep(plain, patches[...].astype(f32).reshape(rows * cols, width))
     gain = gain_ref[...]
     for place, c in enumerate(ORDER):
         parts = [every_nth(plain, 16 * r + c, 64) for r in range(4)]
         tokens[pl.ds(32 * place, 32), :] = normalised(jnp.concatenate(parts, 0), gain)
     few = tokens[: 32 * KEY_COLUMNS]
-    kv_ref[:, :width] = project(few, wk_ref[...])
-    kv_ref[:, width:] = project(few, wv_ref[...])
-    q_ref[...] = project(tokens[...], wq_ref[...])
+    copies[1].wait()
+    kv_ref[...] = project(few, weights[:, width:])
+    q_ref[...] = project(tokens[...], weights[:, :width])
 
 
 def column_of_w(i):
@@ -94,20 +129,24 @@
     return pl.pallas_call(
         own_kernel,
         grid=(1,),
-        in_specs=[whole(patches.shape), whole(gain.shape)] + [column_of_w(i) for i in range(3)],
+        in_specs=[pl.BlockSpec(memory_space=pl.ANY), whole(gain.shape), pl.BlockSpec(memory_space=pl.ANY)],
         out_specs=[whole(s) for s in shapes],
         out_shape=[jax.ShapeDtypeStruct(s, bf16) for s in shapes],
-        scratch_shapes=[pltpu.VMEM((width // 128, count, 128), f32), pltpu.VMEM((count, width), bf16)],
-        compiler_params=pltpu.CompilerParams(vmem_limit_bytes=48 * 2**20),
-        cost_estimate=pl.CostEstimate(flops=1_400_000_000, bytes_accessed=6_000_000, transcendentals=0),
-    )(patches, gain, w_qkv, w_qkv, w_qkv)
-
-
-def halo_tokens(upper_ref, left_ref, corner_ref, gain_ref, plain):
-    keep(plain, left_ref[...].astype(f32))
-    left = jnp.concatenate([every_nth(plain, r, 4) for r in range(4)], 0)
-    rest = jnp.zeros((15, left.shape[1]), f32)
-    every = [left, upper_ref[...].astype(f32), corner_ref[...].astype(f32), rest]
+        scratch_shapes=[
+            pltpu.VMEM(patches.shape, bf16),
+            pltpu.VMEM(w_qkv.shape, bf16),
+            pltpu.VMEM((width // 128, count, 128), f32),
+            pltpu.VMEM((count, width), bf16),
+            pltpu.SemaphoreType.DMA((2,)),
+        ],
+        compiler_params=pltpu.CompilerParams(vmem_limit_bytes=60 * 2**20),
+        cost_estimate=pl.CostEstimate(flops=3_000_000_000, bytes_accessed=6_000_000, transcendentals=0),
+    )(patches, gain, w_qkv)
+
+
+def halo_tokens(upper_ref, left_ref, corner_ref, gain_ref):
+    every = [left_ref[...].astype(f32), upper_ref[...].astype(f32), corner_ref[...].astype(f32)]
+    every.append(jnp.zeros((15, every[0].shape[1]), f32))
     return normalised(jnp.concatenate(every, 0), gain_ref[...])
 
 
@@ -134,8 +173,8 @@
     return total
 
 
-def keyvals_kernel(own_ref, upper_ref, left_ref, corner_ref, gain_ref, wk_ref, wv_ref, pool_ref, out_ref, plain):
-    tokens = halo_tokens(upper_ref, left_ref, corner_ref, gain_ref, plain)
+def keyvals_kernel(own_ref, upper_ref, left_ref, corner_ref, gain_ref, wk_ref, wv_ref, pool_ref, out_ref):
+    tokens = halo_tokens(upper_ref, left_ref, corner_ref, gain_ref)
     width = wk_ref.shape[1]
     both = []
     for part, w_ref in enumerate((wk_ref, wv_ref)):
@@ -149,8 +188,8 @@
         out_ref[g] = jnp.concatenate([p[:, lanes] for p in both], 1).astype(bf16)
 
 
-def queries_kernel(own_ref, upper_ref, left_ref, corner_ref, gain_ref, w_ref, pool_ref, out_ref, plain):
-    tokens = halo_tokens(upper_ref, left_ref, corner_ref, gain_ref, plain)
+def queries_kernel(own_ref, upper_ref, left_ref, corner_ref, gain_ref, w_ref, pool_ref, out_ref):
+    tokens = halo_tokens(upper_ref, left_ref, corner_ref, gain_ref)
     halo = project(tokens, w_ref[...]).astype(f32)
     taps = [pool_ref[t : t + 1, :] for t in range(9)]
     groups = columns_of(own_ref, halo, range(-1, 16))
@@ -172,8 +211,7 @@
         + [whole(taps.shape)],
         out_specs=whole(out_shape),
         out_shape=jax.ShapeDtypeStruct(out_shape, bf16),
-        scratch_shapes=[pltpu.VMEM((gain.shape[1] // 128, 32, 128), f32)],
-        compiler_params=pltpu.CompilerParams(vmem_limit_bytes=48 * 2**20),
+        compiler_params=pltpu.CompilerParams(vmem_limit_bytes=24 * 2**20),
         cost_estimate=pl.CostEstimate(flops=200_000_000, bytes_accessed=4_000_000, transcendentals=0),
     )(own, *halo, gain, *([w_qkv] * len(parts)), taps)
 
@@ -276,11 +314,11 @@
             pltpu.VMEM((16, count), f32),
             pltpu.VMEM((WIDE, count), f32),
         ],
-        compiler_params=pltpu.CompilerParams(vmem_limit_bytes=48 * 2**20),
+        compiler_params=pltpu.CompilerParams(vmem_limit_bytes=24 * 2**20),
         cost_estimate=pl.CostEstimate(
             flops=work * 1024, bytes_accessed=keys * 768, transcendentals=work
         ),
-    )(queries, keyvals, *(carry or ()))
+    )(queries, keyvals, *(() if carry is None else carry))
 
 
 def finish_kernel(parts_ref, w_ref, out_ref, rows):
@@ -312,40 +350,42 @@
         finish_kernel,
         out_shape=jax.ShapeDtypeStruct((16, 8, shape[1]), bf16),
         scratch_shapes=[pltpu.VMEM((shape[1] // 128, shape[0], 128), f32)],
-        compiler_params=pltpu.CompilerParams(vmem_limit_bytes=48 * 2**20),
+        compiler_params=pltpu.CompilerParams(vmem_limit_bytes=24 * 2**20),
     )(parts, w_out)
 
 
 def on_device(patches, norm_gain, w_qkv, pool_q, pool_kv, w_out):
-    upper = passed_along(patches[-1:], ROW)
-    left = passed_along(patches[:, -1:], COL)
-    above_left = corner(patches[-1:, -1:])
+    last_column, last_row, last_token = edges(patches)
+    halo = (passed_along(last_row, ROW), passed_along(last_column, COL), corner(last_token))
     gain = norm_gain[None]
     own_q, own_kv = project_own(patches, gain, w_qkv)
-    halo = (upper[0], left[:, 0], above_left[0])
-    groups = lax.axis_size("zl")
+    groups = lax.axis_size("y")
     flat = pool_call(keyvals_kernel, own_kv, halo, gain, w_qkv, (1, 2), pool_kv, (groups, 32, 2 * WIDE))
-    own = lax.all_to_all(flat, "zl", 0, 0, tiled=True).reshape(-1, 2 * WIDE)
+    own = lax.all_to_all(flat, "y", 0, 0, tiled=True).reshape(-1, 2 * WIDE)
+    own, own_q = lax.optimization_barrier((own, own_q))
+    line = [own, shifted(own, "zq", 2), shifted(own, "zq", 1), shifted(own, "zq", -1)]
     turned = pool_call(queries_kernel, own_q, halo, gain, w_qkv, (0,), pool_q, (2 * groups, WIDE, 128))
-    every_query = lax.all_to_all(turned, ("za", "zl"), 0, 0, tiled=True)
-    line = jnp.concatenate([own, shifted_x(own, 1), shifted_x(own, -1), shifted_x(own, 2)], 0)
+    every_query = lax.all_to_all(turned, ("zc", "y"), 0, 0, tiled=True)
+    line = jnp.concatenate(line, 0)
     swap = lambda block: shifted(block, "core", 1)
-    after, before = shifted(line, "y", 1), shifted(line, "y", -1)
-    half = line.shape[0] // 2
-    far = [shifted(after[:half], "y", 1), shifted(before[half:], "y", -1)]
+    after, before = shifted_x(line, 1), shifted_x(line, -1)
     carry = attend(every_query, line, None, False)
     carry = attend(every_query, swap(line), carry, False)
+    after, before, carry = lax.optimization_barrier((after, before, carry))
+    half = line.shape[0] // 2
+    far = [shifted_x(after[:half], 1), shifted_x(before[half:], -1)]
     for block in (after, swap(after), before, swap(before)):
         carry = attend(every_query, block, carry, False)
+    far, carry = lax.optimization_barrier((far, carry))
     far = jnp.concatenate(far, 0)
     carry = attend(every_query, far, carry, False)
     partial = attend(every_query, swap(far), carry, True)
-    parts = lax.all_to_all(partial, ("za", "zl"), 0, 0, tiled=True)
+    parts = lax.all_to_all(partial, ("zc", "y"), 0, 0, tiled=True)
     return finish(parts, w_out)
 
 
 def solution(mesh):
-    fine = Mesh(mesh.devices.reshape(2, 4, 2, 2, 4, 2), AXES)
+    fine = Mesh(mesh.devices.reshape(4, 2, 2, 2, 4, 2), AXES)
     tiles = P(ROW, COL, None)
     return jax.shard_map(
         on_device,

time: 111 us -> 93.8 us (0.85)
  local copies, waits for them, and re-layouts: 13.5 us -> 2.02 us
  starting transfers between devices: 40.4 us -> 32.5 us
  Pallas kernels: 24.3 us -> 30.2 us
  waiting for transfers between devices: 8.22 us -> 6.41 us
    unnamed x30 -> x20, local copies, waits for them, and re-layouts: 10.1 us -> 1.33 us
    all_to_all x2 -> x1, starting transfers between devices: 11.4 us -> 3.45 us  [on_device(): every_query = lax.all_to_all(turned, ('zc', 'y'), 0, 0, tiled=True)]
    pallas_call x1 -> x2, Pallas kernels: 3.06 us -> 8.22 us  [the longest x1 6.48 us: project_own(): pl.pallas_call(own_kernel, grid=(1,), in_specs=[pl.BlockSpec(memory_space...]
    ppermute x8 -> x7, waiting for transfers between devices: 3.26 us -> 0.02 us  [shifted(): lax.ppermute(block, axis, [(i, (i + distance) % count) for i in range(cou...]
    slice x5 -> x2, local copies, waits for them, and re-layouts: 2.6 us -> 0.04 us  [on_device(): far = [shifted_x(after[:half], 1), shifted_x(before[half:], -1)]]
    ppermute x1, starting transfers between devices: 3.51 us -> 5.51 us  [corner(): return lax.ppermute(block, AXES, route)]
    ppermute x2, starting transfers between devices: 7.7 us -> 5.71 us  [passed_along(): return lax.ppermute(block, axis, [(i - 1, i) for i in range(1, count)])]
    ppermute x8 -> x7, starting transfers between devices: 13.6 us -> 14.9 us  [shifted(): lax.ppermute(block, axis, [(i, (i + distance) % count) for i in range(cou...]
  transfers between devices with their start and end apart: 16 -> 15, of which waited for: 3 -> 3; matrix products, arithmetic and copies ran while one was open for 3% -> 1% of each run, Pallas kernels for 18% -> 26%
where the time goes in v1:
time: 93.8 us; the launch traced here: 93.4 us
  starting transfers between devices  32.5 us (35%)
  Pallas kernels  30.2 us (32%)
  blocking collectives  21.9 us (23%)
  waiting for transfers between devices  6.41 us (7%)
  local copies, waits for them, and re-layouts  2.02 us (2%)
    pallas_call x8, Pallas kernels, attend(): pl.pallas_call(functools.partial(attend_kernel, carry is None, last, bloc...  18.5 us
    ppermute x7, starting transfers between devices, shifted(): lax.ppermute(block, axis, [(i, (i + distance) % count) for i in range(cou...  14.9 us
    all_to_all x1, blocking collectives, on_device(): parts = lax.all_to_all(partial, ('zc', 'y'), 0, 0, tiled=True)  12 us
    all_to_all x1, blocking collectives, on_device(): own = lax.all_to_all(flat, 'y', 0, 0, tiled=True).reshape(-1, 2 * WIDE)  9.88 us
    pallas_call x1, Pallas kernels, project_own(): pl.pallas_call(own_kernel, grid=(1,), in_specs=[pl.BlockSpec(memory_space...  6.48 us
    ppermute x2, starting transfers between devices, passed_along(): return lax.ppermute(block, axis, [(i - 1, i) for i in range(1, count)])  5.71 us
    ppermute x1, starting transfers between devices, corner(): return lax.ppermute(block, AXES, route)  5.51 us
    ppermute x4, waiting for transfers between devices, shifted_x(): return lax.ppermute(block, ('xl', 'xh'), route)  5.24 us
  transfers between devices with their start and end apart: 15, of which 3 were waited for; matrix products, arithmetic and copies ran while one was open for 1% of the time, Pallas kernels for 26%

profile of v1, /device:TPU:1, one launch (start us, length us, event | category | flops | bytes accessed | tf_op | source)
XLA Modules:
  0.0 93.4 jit_solution(4975713680229054057)
XLA Ops:
  0.0 1.7 %shard_map.65 = (bf16[32,768]{1,0:T(8,128)(2,1)}, bf16[16,768]{1,0:T(8,128)(2,1)}, bf16[1,768]{1,0:T(2,128)(2,1)}) custom-call(bf16[32,16,768]{2,1,0:T(8,128)(2,1)} %low_ref.1, bf16[32,16,768]{2,1,0:T(8,128)(2,1)} %low_ref.1), custom_call_target="tpu_custom_call" | custom-call | bytes 1000000 | tf_op jit(solution)/shard_map/pallas_call | solution.py:82
  1.7 5.5 %collective-permute-start.2 = (bf16[1,768]{1,0:T(2,128)(2,1)}, bf16[1,768]{1,0:T(2,128)(2,1)S(1)}, u32[]{:S(2)}, u32[]{:S(2)}) collective-permute-start(bf16[1,768]{1,0:T(2,128)(2,1)} %get-tuple-element.37), channel_id=1, source_target_pairs={{0,17},{1,18},{2,19},{3,20},{4,21},{5,22},{6,23},{7,24},{8,25},{9,... | collective-permute-start | bytes 4616 | tf_op jit(solution)/shard_map/ppermute | solution.py:42
  7.3 3.5 %collective-permute-start = (bf16[16,768]{1,0:T(8,128)(2,1)}, bf16[16,768]{1,0:T(8,128)(2,1)S(1)}, u32[]{:S(2)}, u32[]{:S(2)}) collective-permute-start(bf16[16,768]{1,0:T(8,128)(2,1)} %get-tuple-element.35), channel_id=1, source_target_pairs={{0,16},{16,32},{32,48},{48,64},{64,80},{80,96},{96,112},{112,128},... | collective-permute-start | bytes 73736 | tf_op jit(solution)/shard_map/ppermute | solution.py:36
  10.8 2.2 %collective-permute-start.1 = (bf16[32,768]{1,0:T(8,128)(2,1)}, bf16[32,768]{1,0:T(8,128)(2,1)S(1)}, u32[]{:S(2)}, u32[]{:S(2)}) collective-permute-start(bf16[32,768]{1,0:T(8,128)(2,1)} %get-tuple-element.36), channel_id=1, source_target_pairs={{0,1},{1,2},{2,3},{3,4},{4,5},{5,6},{6,7},{7,8},{8,9},{9,10},{10,1... | collective-permute-start | bytes 147464 | tf_op jit(solution)/shard_map/ppermute | solution.py:36
  13.0 0.6 broadcast_in_dim.3.gain_ref
  13.6 6.5 %shard_map.64 = (bf16[512,768]{1,0:T(8,128)(2,1)}, bf16[352,1536]{1,0:T(8,128)(2,1)}) custom-call(bf16[32,16,768]{2,1,0:T(8,128)(2,1)} %low_ref.1, f32[1,768]{1,0:T(1,128)} %broadcast_in_dim.3.gain_ref, bf16[768,2304]{1,0:T(8,128)(2,1)} %w_ref.4), custom_call_target="tpu_custom_call" | custom-call | flops 3000000000 | bytes 6000000 | tf_op jit(solution)/shard_map/pallas_call | solution.py:129
  20.2 1.2 %copy-done.2 = bf16[352,1536]{1,0:T(8,128)(2,1)S(1)} copy-done((bf16[352,1536]{1,0:T(8,128)(2,1)S(1)}, bf16[352,1536]{1,0:T(8,128)(2,1)}, u32[]{:S(2)}) %copy-start.2) | copy-done | bytes 1081368
  21.4 0.8 shard_map.66
  22.2 9.9 %all_to_all.15 = bf16[4,32,384]{2,1,0:T(8,128)(2,1)S(1)} all-to-all(bf16[4,32,384]{2,1,0:T(8,128)(2,1)S(1)} %shard_map.66), channel_id=1, replica_groups=mesh['zq'=4,'zc'=2,'xl'=2,'xh'=2,'y'=4,'core'=2] {'y'}, dimensions={0} | all-to-all | bytes 196608 | tf_op jit(solution)/shard_map/all_to_all | solution.py:364
  32.1 5.1 %collective-permute-start.5 = (bf16[128,384]{1,0:T(8,128)(2,1)S(1)}, bf16[128,384]{1,0:T(8,128)(2,1)S(1)}, u32[]{:S(2)}, u32[]{:S(2)}) collective-permute-start(bf16[128,384]{1,0:T(8,128)(2,1)S(1)} %bitcast.1), channel_id=1, source_target_pairs={{0,192},{64,0},{128,64},{192,128},{1,193},{65,1},{129,65},{193,129... | collective-permute-start | bytes 294920 | tf_op jit(solution)/shard_map/ppermute | solution.py:25
  37.2 3.3 %collective-permute-start.3 = (bf16[128,384]{1,0:T(8,128)(2,1)S(1)}, bf16[128,384]{1,0:T(8,128)(2,1)S(1)}, u32[]{:S(2)}, u32[]{:S(2)}) collective-permute-start(bf16[128,384]{1,0:T(8,128)(2,1)S(1)} %bitcast.3), channel_id=1, source_target_pairs={{0,128},{64,192},{128,0},{192,64},{1,129},{65,193},{129,1},{193,65... | collective-permute-start | bytes 294920 | tf_op jit(solution)/shard_map/ppermute | solution.py:25
  40.5 1.5 %shard_map.67 = bf16[8,192,128]{2,1,0:T(8,128)(2,1)} custom-call(bf16[512,768]{1,0:T(8,128)(2,1)S(1)} %copy-done.3, bf16[16,768]{1,0:T(8,128)(2,1)S(1)} %collective-permute-done.upper_ref, bf16[32,768]{1,0:T(8,128)(2,1)S(1)} %collective-permute-done.1.left_ref, bf16[1,768]{1,0:T(2,128)(2,1)S(1)} %collective-permute-done.2.corner_ref, ...), custom_call_target="tpu_custom_call" | custom-call | flops 200000000 | bytes 4000000 | tf_op jit(solution)/shard_map/pallas_call | solution.py:206
  42.0 3.5 %all-to-all-start.1 = ((bf16[8,192,128]{2,1,0:T(8,128)(2,1)}), bf16[8,192,128]{2,1,0:T(8,128)(2,1)S(1)}, u32[]{:S(2)}, u32[]{:S(2)}) async-start(bf16[8,192,128]{2,1,0:T(8,128)(2,1)} %shard_map.67), calls=%async_computation.1 | async-start | bytes 786432 | tf_op jit(solution)/shard_map/all_to_all | solution.py:368
  45.6 3.9 %collective-permute-start.8 = (bf16[512,384]{1,0:T(8,128)(2,1)S(1)}, bf16[512,384]{1,0:T(8,128)(2,1)S(1)}, u32[]{:S(2)}, u32[]{:S(2)}) collective-permute-start(bf16[512,384]{1,0:T(8,128)(2,1)S(1)} %constant_dynamic-update-slice_fusion.kv_ref), channel_id=1, source_target_pairs={{0,1},{1,0},{2,3},{3,2},{4,5},{5,4},{6,7},{7,6},{8,9},{9,8},{10,11... | collective-permute-start | bytes 1179656 | tf_op jit(solution)/shard_map/ppermute | solution.py:25
  49.5 0.9 collective-permute-start.7
  50.4 0.6 collective-permute-start.6
  51.0 1.1 %all-to-all-done.1.q_ref = bf16[8,192,128]{2,1,0:T(8,128)(2,1)S(1)} async-done(((bf16[8,192,128]{2,1,0:T(8,128)(2,1)}), bf16[8,192,128]{2,1,0:T(8,128)(2,1)S(1)}, u32[]{:S(2)}, u32[]{:S(2)}) %all-to-all-start.1) | async-done | bytes 393248 | tf_op jit(solution)/shard_map/all_to_all | solution.py:368
  52.1 2.3 %shard_map.68 = (f32[16,1024]{1,0:T(8,128)S(1)}, f32[192,1024]{1,0:T(8,128)S(1)}) custom-call(bf16[8,192,128]{2,1,0:T(8,128)(2,1)S(1)} %all-to-all-done.1.q_ref, bf16[512,384]{1,0:T(8,128)(2,1)S(1)} %constant_dynamic-update-slice_fusion.kv_ref), custom_call_target="tpu_custom_call" | custom-call | flops 1610612736 | bytes 393216 | tf_op jit(solution)/shard_map/pallas_call | solution.py:305
  54.4 2.3 %shard_map.69 = (f32[16,1024]{1,0:T(8,128)S(1)}, f32[192,1024]{1,0:T(8,128)S(1)}) custom-call(bf16[8,192,128]{2,1,0:T(8,128)(2,1)S(1)} %all-to-all-done.1.q_ref, bf16[512,384]{1,0:T(8,128)(2,1)S(1)} %collective-permute-done.8.kv_ref, f32[16,1024]{1,0:T(8,128)S(1)} %get-tuple-element.41.refs_0_, f32[192,1024]{1,0:T(8,128)S(1)} %get-tuple-element.42.refs_1_), custom_call_target="tpu_custom_call" | custom-call | flops 1610612736 | bytes 393216 | tf_op jit(solution)/shard_map/pallas_call | solution.py:305
  56.7 3.4 %collective-permute-done.7.kv_ref = bf16[512,384]{1,0:T(8,128)(2,1)S(1)} collective-permute-done((bf16[512,384]{1,0:T(8,128)(2,1)S(1)}, bf16[512,384]{1,0:T(8,128)(2,1)S(1)}, u32[]{:S(2)}, u32[]{:S(2)}) %collective-permute-start.7) | collective-permute-done | bytes 393248 | tf_op jit(solution)/shard_map/ppermute | solution.py:31
  60.2 1.8 %collective-permute-done.6.kv_ref = bf16[512,384]{1,0:T(8,128)(2,1)S(1)} collective-permute-done((bf16[512,384]{1,0:T(8,128)(2,1)S(1)}, bf16[512,384]{1,0:T(8,128)(2,1)S(1)}, u32[]{:S(2)}, u32[]{:S(2)}) %collective-permute-start.6) | collective-permute-done | bytes 393248 | tf_op jit(solution)/shard_map/ppermute | solution.py:31
  62.0 1.2 %collective-permute-start.12 = (bf16[512,384]{1,0:T(8,128)(2,1)S(1)}, bf16[512,384]{1,0:T(8,128)(2,1)S(1)}, u32[]{:S(2)}, u32[]{:S(2)}) collective-permute-start(bf16[512,384]{1,0:T(8,128)(2,1)S(1)} %collective-permute-done.6.kv_ref), channel_id=1, source_target_pairs={{0,1},{1,0},{2,3},{3,2},{4,5},{5,4},{6,7},{7,6},{8,9},{9,8},{10,11... | collective-permute-start | bytes 1179656 | tf_op jit(solution)/shard_map/ppermute | solution.py:25
  63.4 1.5 %collective-permute-start.9 = (bf16[256,384]{1,0:T(8,128)(2,1)S(1)}, bf16[256,384]{1,0:T(8,128)(2,1)S(1)}, u32[]{:S(2)}, u32[]{:S(2)}) collective-permute-start(bf16[256,384]{1,0:T(8,128)(2,1)S(1)} %slice.6), channel_id=1, source_target_pairs={{0,16},{16,8},{8,24},{24,0},{1,17},{17,9},{9,25},{25,1},{2,18},{18... | collective-permute-start | bytes 589832 | tf_op jit(solution)/shard_map/ppermute | solution.py:31
  64.8 2.3 %shard_map.70 = (f32[16,1024]{1,0:T(8,128)S(1)}, f32[192,1024]{1,0:T(8,128)S(1)}) custom-call(bf16[8,192,128]{2,1,0:T(8,128)(2,1)S(1)} %all-to-all-done.1.q_ref, bf16[512,384]{1,0:T(8,128)(2,1)S(1)} %collective-permute-done.6.kv_ref, f32[16,1024]{1,0:T(8,128)S(1)} %get-tuple-element.47.refs_0_, f32[192,1024]{1,0:T(8,128)S(1)} %get-tuple-element.48.refs_1_), custom_call_target="tpu_custom_call" | custom-call | flops 1610612736 | bytes 393216 | tf_op jit(solution)/shard_map/pallas_call | solution.py:305
  67.1 2.3 %shard_map.71 = (f32[16,1024]{1,0:T(8,128)S(1)}, f32[192,1024]{1,0:T(8,128)S(1)}) custom-call(bf16[8,192,128]{2,1,0:T(8,128)(2,1)S(1)} %all-to-all-done.1.q_ref, bf16[512,384]{1,0:T(8,128)(2,1)S(1)} %collective-permute-done.12.kv_ref, f32[16,1024]{1,0:T(8,128)S(1)} %get-tuple-element.49.refs_0_, f32[192,1024]{1,0:T(8,128)S(1)} %get-tuple-element.50.refs_1_), custom_call_target="tpu_custom_call" | custom-call | flops 1610612736 | bytes 393216 | tf_op jit(solution)/shard_map/pallas_call | solution.py:305
  69.5 2.3 %shard_map.72 = (f32[16,1024]{1,0:T(8,128)S(1)}, f32[192,1024]{1,0:T(8,128)S(1)}) custom-call(bf16[8,192,128]{2,1,0:T(8,128)(2,1)S(1)} %all-to-all-done.1.q_ref, bf16[512,384]{1,0:T(8,128)(2,1)S(1)} %collective-permute-done.7.kv_ref, f32[16,1024]{1,0:T(8,128)S(1)} %get-tuple-element.51.refs_0_, f32[192,1024]{1,0:T(8,128)S(1)} %get-tuple-element.52.refs_1_), custom_call_target="tpu_custom_call" | custom-call | flops 1610612736 | bytes 393216 | tf_op jit(solution)/shard_map/pallas_call | solution.py:305
  71.8 2.3 %shard_map.73 = (f32[16,1024]{1,0:T(8,128)S(1)}, f32[192,1024]{1,0:T(8,128)S(1)}) custom-call(bf16[8,192,128]{2,1,0:T(8,128)(2,1)S(1)} %all-to-all-done.1.q_ref, bf16[512,384]{1,0:T(8,128)(2,1)S(1)} %collective-permute-done.11.kv_ref, f32[16,1024]{1,0:T(8,128)S(1)} %get-tuple-element.53.refs_0_, f32[192,1024]{1,0:T(8,128)S(1)} %get-tuple-element.54.refs_1_), custom_call_target="tpu_custom_call" | custom-call | flops 1610612736 | bytes 393216 | tf_op jit(solution)/shard_map/pallas_call | solution.py:305
  74.2 1.3 %collective-permute-start.13 = (bf16[512,384]{1,0:T(8,128)(2,1)S(1)}, bf16[512,384]{1,0:T(8,128)(2,1)S(1)}, u32[]{:S(2)}, u32[]{:S(2)}) collective-permute-start(bf16[512,384]{1,0:T(8,128)(2,1)S(1)} %constant_dynamic-update-slice_fusion.4.kv_ref), channel_id=1, source_target_pairs={{0,1},{1,0},{2,3},{3,2},{4,5},{5,4},{6,7},{7,6},{8,9},{9,8},{10,11... | collective-permute-start | bytes 1179656 | tf_op jit(solution)/shard_map/ppermute | solution.py:25
  75.5 2.3 %shard_map.74 = (f32[16,1024]{1,0:T(8,128)S(1)}, f32[192,1024]{1,0:T(8,128)S(1)}) custom-call(bf16[8,192,128]{2,1,0:T(8,128)(2,1)S(1)} %all-to-all-done.1.q_ref, bf16[512,384]{1,0:T(8,128)(2,1)S(1)} %constant_dynamic-update-slice_fusion.4.kv_ref, f32[16,1024]{1,0:T(8,128)S(1)} %get-tuple-element.59.refs_0_, f32[192,1024]{1,0:T(8,128)S(1)} %get-tuple-element.60.refs_1_), custom_call_target="tpu_custom_call" | custom-call | flops 1610612736 | bytes 393216 | tf_op jit(solution)/shard_map/pallas_call | solution.py:305
  77.9 2.4 %shard_map.75 = bf16[8,208,128]{2,1,0:T(8,128)(2,1)S(1)} custom-call(bf16[8,192,128]{2,1,0:T(8,128)(2,1)S(1)} %all-to-all-done.1.q_ref, bf16[512,384]{1,0:T(8,128)(2,1)S(1)} %collective-permute-done.13.kv_ref, f32[16,1024]{1,0:T(8,128)S(1)} %get-tuple-element.61.refs_0_, f32[192,1024]{1,0:T(8,128)S(1)} %get-tuple-element.62.refs_1_), custom_call_target="tpu_custom_call" | custom-call | flops 1610612736 | bytes 393216 | tf_op jit(solution)/shard_map/pallas_call | solution.py:305
  80.2 12.0 %all_to_all.16.parts_ref = bf16[8,208,128]{2,1,0:T(8,128)(2,1)S(1)} all-to-all(bf16[8,208,128]{2,1,0:T(8,128)(2,1)S(1)} %shard_map.75), channel_id=1, replica_groups=mesh['zq'=4,'zc'=2,'xl'=2,'xh'=2,'y'=4,'core'=2] {'zc','y'}, dimensions={0} | all-to-all | bytes 851968 | tf_op jit(solution)/shard_map/all_to_all | solution.py:383
  92.2 1.1 %shard_map.76 = bf16[16,8,768]{2,1,0:T(8,128)(2,1)} custom-call(bf16[8,208,128]{2,1,0:T(8,128)(2,1)S(1)} %all_to_all.16.parts_ref, bf16[768,768]{1,0:T(8,128)(2,1)S(1)} %copy-done.1), custom_call_target="tpu_custom_call" | custom-call | tf_op jit(solution)/shard_map/pallas_call | solution.py:349
  (38 shorter events, 0.4 us)
Async XLA Ops:
  0.0 13.0 %copy-start.7 = (f32[768]{0:T(1024)S(1)}, f32[768]{0:T(1024)}, u32[]{:S(2)}) copy-start(f32[768]{0:T(1024)} %param.7) | copy-start | bytes 9220
  1.7 18.3 %collective-permute-start.2 = (bf16[1,768]{1,0:T(2,128)(2,1)}, bf16[1,768]{1,0:T(2,128)(2,1)S(1)}, u32[]{:S(2)}, u32[]{:S(2)}) collective-permute-start(bf16[1,768]{1,0:T(2,128)(2,1)} %get-tuple-element.37), channel_id=1, source_target_pairs={{0,17},{1,18},{2,19},{3,20},{4,21},{5,22},{6,23},{7,24},{8,25},{9,... | collective-permute-start | bytes 4616 | tf_op jit(solution)/shard_map/ppermute | solution.py:42
  7.3 12.8 %collective-permute-start = (bf16[16,768]{1,0:T(8,128)(2,1)}, bf16[16,768]{1,0:T(8,128)(2,1)S(1)}, u32[]{:S(2)}, u32[]{:S(2)}) collective-permute-start(bf16[16,768]{1,0:T(8,128)(2,1)} %get-tuple-element.35), channel_id=1, source_target_pairs={{0,16},{16,32},{32,48},{48,64},{64,80},{80,96},{96,112},{112,128},... | collective-permute-start | bytes 73736 | tf_op jit(solution)/shard_map/ppermute | solution.py:36
  10.8 9.3 %collective-permute-start.1 = (bf16[32,768]{1,0:T(8,128)(2,1)}, bf16[32,768]{1,0:T(8,128)(2,1)S(1)}, u32[]{:S(2)}, u32[]{:S(2)}) collective-permute-start(bf16[32,768]{1,0:T(8,128)(2,1)} %get-tuple-element.36), channel_id=1, source_target_pairs={{0,1},{1,2},{2,3},{3,4},{4,5},{5,6},{6,7},{7,8},{8,9},{9,10},{10,1... | collective-permute-start | bytes 147464 | tf_op jit(solution)/shard_map/ppermute | solution.py:36
  13.6 6.5 %copy-start = (bf16[768,2304]{1,0:T(8,128)(2,1)S(1)}, bf16[768,2304]{1,0:T(8,128)(2,1)}, u32[]{:S(2)}) copy-start(bf16[768,2304]{1,0:T(8,128)(2,1)} %w_ref.4) | copy-start | bytes 10616836
  13.6 6.5 %copy-start.4 = (f32[9,1536]{1,0:T(8,128)S(1)}, f32[9,1536]{1,0:T(8,128)}, u32[]{:S(2)}) copy-start(f32[9,1536]{1,0:T(8,128)} %pool_ref.2) | copy-start | bytes 165892
  13.6 6.5 %copy-start.6 = (f32[1,768]{1,0:T(1,128)S(1)}, f32[1,768]{1,0:T(1,128)}, u32[]{:S(2)}) copy-start(f32[1,768]{1,0:T(1,128)} %broadcast_in_dim.3.gain_ref) | copy-start | bytes 9220
  20.1 1.2 %copy-start.2 = (bf16[352,1536]{1,0:T(8,128)(2,1)S(1)}, bf16[352,1536]{1,0:T(8,128)(2,1)}, u32[]{:S(2)}) copy-start(bf16[352,1536]{1,0:T(8,128)(2,1)} %get-tuple-element.34.own_ref) | copy-start | bytes 3244036
  21.4 19.1 %copy-start.3 = (bf16[512,768]{1,0:T(8,128)(2,1)S(1)}, bf16[512,768]{1,0:T(8,128)(2,1)}, u32[]{:S(2)}) copy-start(bf16[512,768]{1,0:T(8,128)(2,1)} %get-tuple-element.39.own_ref) | copy-start | bytes 2359300
  21.4 19.1 %copy-start.5 = (f32[9,768]{1,0:T(8,128)S(1)}, f32[9,768]{1,0:T(8,128)}, u32[]{:S(2)}) copy-start(f32[9,768]{1,0:T(8,128)} %pool_ref.3) | copy-start | bytes 82948
  32.1 13.5 %collective-permute-start.5 = (bf16[128,384]{1,0:T(8,128)(2,1)S(1)}, bf16[128,384]{1,0:T(8,128)(2,1)S(1)}, u32[]{:S(2)}, u32[]{:S(2)}) collective-permute-start(bf16[128,384]{1,0:T(8,128)(2,1)S(1)} %bitcast.1), channel_id=1, source_target_pairs={{0,192},{64,0},{128,64},{192,128},{1,193},{65,1},{129,65},{193,129... | collective-permute-start | bytes 294920 | tf_op jit(solution)/shard_map/ppermute | solution.py:25
  37.2 8.3 %collective-permute-start.4 = (bf16[128,384]{1,0:T(8,128)(2,1)S(1)}, bf16[128,384]{1,0:T(8,128)(2,1)S(1)}, u32[]{:S(2)}, u32[]{:S(2)}) collective-permute-start(bf16[128,384]{1,0:T(8,128)(2,1)S(1)} %bitcast.2), channel_id=1, source_target_pairs={{0,64},{64,128},{128,192},{192,0},{1,65},{65,129},{129,193},{193,1... | collective-permute-start | bytes 294920 | tf_op jit(solution)/shard_map/ppermute | solution.py:25
  37.2 8.3 %collective-permute-start.3 = (bf16[128,384]{1,0:T(8,128)(2,1)S(1)}, bf16[128,384]{1,0:T(8,128)(2,1)S(1)}, u32[]{:S(2)}, u32[]{:S(2)}) collective-permute-start(bf16[128,384]{1,0:T(8,128)(2,1)S(1)} %bitcast.3), channel_id=1, source_target_pairs={{0,128},{64,192},{128,0},{192,64},{1,129},{65,193},{129,1},{193,65... | collective-permute-start | bytes 294920 | tf_op jit(solution)/shard_map/ppermute | solution.py:25
  42.0 10.1 %all-to-all-start.1 = ((bf16[8,192,128]{2,1,0:T(8,128)(2,1)}), bf16[8,192,128]{2,1,0:T(8,128)(2,1)S(1)}, u32[]{:S(2)}, u32[]{:S(2)}) async-start(bf16[8,192,128]{2,1,0:T(8,128)(2,1)} %shard_map.67), calls=%async_computation.1 | async-start | bytes 786432 | tf_op jit(solution)/shard_map/all_to_all | solution.py:368
  45.6 8.8 %collective-permute-start.8 = (bf16[512,384]{1,0:T(8,128)(2,1)S(1)}, bf16[512,384]{1,0:T(8,128)(2,1)S(1)}, u32[]{:S(2)}, u32[]{:S(2)}) collective-permute-start(bf16[512,384]{1,0:T(8,128)(2,1)S(1)} %constant_dynamic-update-slice_fusion.kv_ref), channel_id=1, source_target_pairs={{0,1},{1,0},{2,3},{3,2},{4,5},{5,4},{6,7},{7,6},{8,9},{9,8},{10,11... | collective-permute-start | bytes 1179656 | tf_op jit(solution)/shard_map/ppermute | solution.py:25
  49.5 10.7 %collective-permute-start.7 = (bf16[512,384]{1,0:T(8,128)(2,1)S(1)}, bf16[512,384]{1,0:T(8,128)(2,1)S(1)}, u32[]{:S(2)}, u32[]{:S(2)}) collective-permute-start(bf16[512,384]{1,0:T(8,128)(2,1)S(1)} %constant_dynamic-update-slice_fusion.kv_ref), channel_id=1, source_target_pairs={{0,24},{16,0},{8,16},{24,8},{1,25},{17,1},{9,17},{25,9},{2,26},{18... | collective-permute-start | bytes 1179656 | tf_op jit(solution)/shard_map/ppermute | solution.py:31
  50.4 11.6 %collective-permute-start.6 = (bf16[512,384]{1,0:T(8,128)(2,1)S(1)}, bf16[512,384]{1,0:T(8,128)(2,1)S(1)}, u32[]{:S(2)}, u32[]{:S(2)}) collective-permute-start(bf16[512,384]{1,0:T(8,128)(2,1)S(1)} %constant_dynamic-update-slice_fusion.kv_ref), channel_id=1, source_target_pairs={{0,16},{16,8},{8,24},{24,0},{1,17},{17,9},{9,25},{25,1},{2,18},{18... | collective-permute-start | bytes 1179656 | tf_op jit(solution)/shard_map/ppermute | solution.py:31
  62.0 5.2 %collective-permute-start.12 = (bf16[512,384]{1,0:T(8,128)(2,1)S(1)}, bf16[512,384]{1,0:T(8,128)(2,1)S(1)}, u32[]{:S(2)}, u32[]{:S(2)}) collective-permute-start(bf16[512,384]{1,0:T(8,128)(2,1)S(1)} %collective-permute-done.6.kv_ref), channel_id=1, source_target_pairs={{0,1},{1,0},{2,3},{3,2},{4,5},{5,4},{6,7},{7,6},{8,9},{9,8},{10,11... | collective-permute-start | bytes 1179656 | tf_op jit(solution)/shard_map/ppermute | solution.py:25
  63.2 8.6 %collective-permute-start.11 = (bf16[512,384]{1,0:T(8,128)(2,1)S(1)}, bf16[512,384]{1,0:T(8,128)(2,1)S(1)}, u32[]{:S(2)}, u32[]{:S(2)}) collective-permute-start(bf16[512,384]{1,0:T(8,128)(2,1)S(1)} %collective-permute-done.7.kv_ref), channel_id=1, source_target_pairs={{0,1},{1,0},{2,3},{3,2},{4,5},{5,4},{6,7},{7,6},{8,9},{9,8},{10,11... | collective-permute-start | bytes 1179656 | tf_op jit(solution)/shard_map/ppermute | solution.py:25
  63.3 10.8 %collective-permute-start.10 = (bf16[256,384]{1,0:T(8,128)(2,1)S(1)}, bf16[256,384]{1,0:T(8,128)(2,1)S(1)}, u32[]{:S(2)}, u32[]{:S(2)}) collective-permute-start(bf16[256,384]{1,0:T(8,128)(2,1)S(1)} %slice.7), channel_id=1, source_target_pairs={{0,24},{16,0},{8,16},{24,8},{1,25},{17,1},{9,17},{25,9},{2,26},{18... | collective-permute-start | bytes 589832 | tf_op jit(solution)/shard_map/ppermute | solution.py:31
  63.4 10.7 %collective-permute-start.9 = (bf16[256,384]{1,0:T(8,128)(2,1)S(1)}, bf16[256,384]{1,0:T(8,128)(2,1)S(1)}, u32[]{:S(2)}, u32[]{:S(2)}) collective-permute-start(bf16[256,384]{1,0:T(8,128)(2,1)S(1)} %slice.6), channel_id=1, source_target_pairs={{0,16},{16,8},{8,24},{24,0},{1,17},{17,9},{9,25},{25,1},{2,18},{18... | collective-permute-start | bytes 589832 | tf_op jit(solution)/shard_map/ppermute | solution.py:31
  74.2 3.7 %collective-permute-start.13 = (bf16[512,384]{1,0:T(8,128)(2,1)S(1)}, bf16[512,384]{1,0:T(8,128)(2,1)S(1)}, u32[]{:S(2)}, u32[]{:S(2)}) collective-permute-start(bf16[512,384]{1,0:T(8,128)(2,1)S(1)} %constant_dynamic-update-slice_fusion.4.kv_ref), channel_id=1, source_target_pairs={{0,1},{1,0},{2,3},{3,2},{4,5},{5,4},{6,7},{7,6},{8,9},{9,8},{10,11... | collective-permute-start | bytes 1179656 | tf_op jit(solution)/shard_map/ppermute | solution.py:25
  77.8 14.4 %copy-start.1 = (bf16[768,768]{1,0:T(8,128)(2,1)S(1)}, bf16[768,768]{1,0:T(8,128)(2,1)}, u32[]{:S(2)}) copy-start(bf16[768,768]{1,0:T(8,128)(2,1)} %w_ref.5) | copy-start | bytes 3538948

commit v2 on v0

v2 whole, which is shorter than its diff:
```python
import functools
import math

import jax
import jax.numpy as jnp
from jax import lax
from jax.experimental import pallas as pl
from jax.experimental.pallas import tpu as pltpu
from jax.sharding import Mesh
from jax.sharding import PartitionSpec as P

AXES = ("zq", "zc", "xl", "xh", "y", "core")
ROW = ("zq", "zc", "xl")
COL = ("xh", "y", "core")
HEAD = 64
GROUP = 3
WIDE = GROUP * HEAD
SCALE = HEAD**-0.5 * math.log2(math.e)
STATS = 16
bf16, f32 = jnp.bfloat16, jnp.float32


def shifted(block, axis, distance):
    count = lax.axis_size(axis)
    return lax.ppermute(block, axis, [(i, (i + distance) % count) for i in range(count)])


def shifted_x(block, distance):
    place = lambda i: (i % 2) * 2 + i // 2
    route = [(place(i), place((i + distance) % 4)) for i in range(4)]
    return lax.ppermute(block, ("xl", "xh"), route)


def passed_along(block, axis):
    count = lax.axis_size(axis)
    return lax.ppermute(block, axis, [(i - 1, i) for i in range(1, count)])


def corner(block):
    rows, cols = lax.axis_size(ROW), lax.axis_size(COL)
    route = [((r - 1) * cols + c - 1, r * cols + c) for r in range(1, rows) for c in range(1, cols)]
    return lax.ppermute(block, AXES, route)


def normalised(values, gain):
    center = values - jnp.mean(values, axis=-1, keepdims=True)
    spread = jnp.mean(center * center, axis=-1, keepdims=True)
    return center * lax.rsqrt(spread + 1e-06) * gain


def project(tokens, weights):
    return jnp.dot(tokens, weights, preferred_element_type=f32).astype(bf16)


ORDER = (0, 1, 3, 4, 5, 7, 8, 9, 11, 12, 13, 2, 6, 10, 14, 15)
KEY_COLUMNS = 11


def keep(plain, values):
    for k in range(plain.shape[0]):
        plain[k] = values[:, 128 * k : 128 * (k + 1)]


def every_nth(plain, start, step):
    picked = [plain[k, pl.ds(start, 8, stride=step), :] for k in range(plain.shape[0])]
    return jnp.concatenate(picked, 1)


def tokens_kernel(patches_ref, gain_ref, tokens_ref, column_ref, row_ref, corner_ref, plain):
    rows, cols, width = patches_ref.shape
    keep(plain, patches_ref[...].astype(f32).reshape(rows * cols, width))
    gain = gain_ref[...]
    last = [None] * cols
    for place, c in enumerate(ORDER):
        parts = [every_nth(plain, cols * r + c, 4 * cols) for r in range(4)]
        column = normalised(jnp.concatenate(parts, 0), gain)
        tokens_ref[pl.ds(32 * place, 32), :] = column.astype(bf16)
        last[c] = column[31:]
    column_ref[...] = column.astype(bf16)
    row_ref[...] = jnp.concatenate(last, 0).astype(bf16)
    corner_ref[...] = last[-1].astype(bf16)


def whole(shape):
    return pl.BlockSpec(shape, lambda *_: (0,) * len(shape))


def normalised_tokens(patches, gain):
    rows, cols, width = patches.shape
    shapes = [(rows * cols, width), (rows, width), (cols, width), (1, width)]
    return pl.pallas_call(
        tokens_kernel,
        in_specs=[pl.BlockSpec(memory_space=pltpu.VMEM)] * 2,
        out_specs=[pl.BlockSpec(memory_space=pltpu.VMEM)] * 4,
        out_shape=[jax.ShapeDtypeStruct(s, bf16) for s in shapes],
        scratch_shapes=[pltpu.VMEM((width // 128, rows * cols, 128), f32)],
        compiler_params=pltpu.CompilerParams(vmem_limit_bytes=16 * 2**20),
        cost_estimate=pl.CostEstimate(flops=4_000_000_000, bytes_accessed=1_000_000, transcendentals=0),
    )(patches, gain)


def halo_tokens(upper_ref, left_ref, corner_ref):
    rest = jnp.zeros((15, left_ref.shape[1]), f32)
    every = [left_ref[...].astype(f32), upper_ref[...].astype(f32), corner_ref[...].astype(f32), rest]
    return jnp.concatenate(every, 0).astype(bf16)


def columns_of(own, halo, columns):
    first = lax.broadcasted_iota(jnp.int32, (8, own.shape[1]), 0) == 0
    groups = {}
    for c in columns:
        if c < 0:
            block, above = halo[0:32], halo[48:49]
        else:
            place = ORDER.index(c)
            block, above = own[32 * place : 32 * place + 32].astype(f32), halo[32 + c : 33 + c]
        four = [block[8 * r : 8 * r + 8] for r in range(4)]
        groups[c] = [jnp.where(first, above, pltpu.roll(four[3], 1, 0))] + four
    return groups


def pooled(groups, taps, column, row):
    total = None
    for a in range(3):
        for b in range(3):
            term = taps[3 * a + b] * groups[column + b - 1][row + a]
            total = term if total is None else total + term
    return total


def keyvals_kernel(tokens_ref, upper_ref, left_ref, corner_ref, w_ref, pool_ref, out_ref):
    halo_in = halo_tokens(upper_ref, left_ref, corner_ref)
    width = tokens_ref.shape[1]
    both = []
    for part in range(2):
        cols = pl.ds(part * width, width)
        weights = w_ref[:, (part + 1) * width : (part + 2) * width]
        halo = project(halo_in, weights).astype(f32)
        own = project(tokens_ref[: 32 * KEY_COLUMNS], weights)
        taps = [pool_ref[t : t + 1, cols] for t in range(9)]
        groups = columns_of(own, halo, (-1,) + ORDER[:KEY_COLUMNS])
        both.append(jnp.concatenate([pooled(groups, taps, 4 * j, 0) for j in range(4)], 0))
    count = width // WIDE
    for g in range(count):
        lanes = slice(g * WIDE, (g + 1) * WIDE)
        block = jnp.concatenate([p[:, lanes] for p in both], 1).astype(bf16)
        for copy in range(out_ref.shape[0] // count):
            out_ref[copy * count + g] = block


def queries_kernel(tokens_ref, upper_ref, left_ref, corner_ref, w_ref, pool_ref, out_ref):
    width = tokens_ref.shape[1]
    weights = w_ref[:, :width]
    halo = project(halo_tokens(upper_ref, left_ref, corner_ref), weights).astype(f32)
    own = project(tokens_ref[...], weights)
    taps = [pool_ref[t : t + 1, :] for t in range(9)]
    groups = columns_of(own, halo, range(-1, 16))
    rows = [pooled(groups, taps, 2 * j, 2 * p) for j in range(8) for p in range(2)]
    turned = jnp.concatenate(rows, 0).T.astype(bf16)
    count = width // WIDE
    for g in range(count):
        block = turned[g * WIDE : (g + 1) * WIDE]
        for copy in range(out_ref.shape[0] // count):
            out_ref[copy * count + g] = block


def pool_call(kernel, tokens, halo, w_qkv, taps, out_shape):
    return pl.pallas_call(
        kernel,
        in_specs=[pl.BlockSpec(memory_space=pltpu.VMEM)] * (3 + len(halo)),
        out_specs=pl.BlockSpec(memory_space=pltpu.VMEM),
        out_shape=jax.ShapeDtypeStruct(out_shape, bf16),
        compiler_params=pltpu.CompilerParams(vmem_limit_bytes=24 * 2**20),
        cost_estimate=pl.CostEstimate(flops=1_500_000_000, bytes_accessed=4_000_000, transcendentals=0),
    )(tokens, *halo, w_qkv, taps)


def attend_kernel(first, last, block, qb, q_ref, kv_ref, *refs):
    if first:
        stat_in, acc_in = None, None
    else:
        stat_in, acc_in, *refs = refs
    if last:
        out_ref, qz, stat, acc = refs
    else:
        stat, acc, qz = refs
    tiles = q_ref.shape[0]
    count = tiles * 128
    zero = jnp.zeros((HEAD, 128), bf16)
    for t in range(tiles):
        lanes = slice(t * 128, (t + 1) * 128)
        for h in range(GROUP):
            here = HEAD * (h % 2)
            qz[h, here : here + HEAD, lanes] = q_ref[t, HEAD * h : HEAD * (h + 1)]
            qz[h, HEAD - here : 2 * HEAD - here, lanes] = zero

    jobs = [
        (k, j, h)
        for k in range(kv_ref.shape[0] // block)
        for j in range(count // qb)
        for h in range(GROUP)
    ]
    ones = jnp.ones((16, block), bf16)
    values = [kv_ref[pl.ds(k * block, block), 128:384].T for k in range(kv_ref.shape[0] // block)]

    def scores(k, j, h):
        keys = kv_ref[pl.ds(k * block, block), 128 * (h // 2) : 128 * (h // 2) + 128]
        return jnp.dot(keys, qz[h, :, j * qb : (j + 1) * qb], preferred_element_type=f32)

    ready = scores(*jobs[0])
    for place, (k, j, h) in enumerate(jobs):
        now = ready
        if place + 1 < len(jobs):
            ready = scores(*jobs[place + 1])
        lanes = slice(j * qb, (j + 1) * qb)
        rows = slice(HEAD * h, HEAD * (h + 1))
        new = jnp.max(now, axis=0, keepdims=True)
        source = (stat_in, acc_in) if k == 0 else (stat, acc)
        carried = k > 0 or not first
        if carried:
            old = source[0][h : h + 1, lanes]
            new = jnp.maximum(old, new)
        weights = jnp.exp2((now - new) * SCALE).astype(bf16)
        value = jnp.concatenate([values[k][HEAD * (h + 1) : HEAD * (h + 2)], ones], 0)
        part = jnp.dot(value, weights, preferred_element_type=f32)
        total, numer = part[HEAD : HEAD + 1], part[:HEAD]
        if carried:
            factor = jnp.exp2((old - new) * SCALE)
            total = source[0][8 + h : 9 + h, lanes] * factor + total
            numer = source[1][rows, lanes] * factor + numer
        stat[h : h + 1, lanes] = new
        stat[8 + h : 9 + h, lanes] = total
        acc[rows, lanes] = numer

    if last:
        total = stat[8 : 8 + GROUP]
        logs = stat[0:GROUP] * SCALE + jnp.log2(total)
        high = logs.astype(bf16)
        left = logs - high.astype(f32)
        middle = left.astype(bf16)
        low = left - middle.astype(f32)
        three = [high.astype(f32), middle.astype(f32), low]
        packed = jnp.concatenate(three + [jnp.zeros((STATS - 9, count), f32)], 0).astype(bf16)
        for t in range(tiles):
            lanes = slice(t * 128, (t + 1) * 128)
            for h in range(GROUP):
                rows = slice(HEAD * h, HEAD * (h + 1))
                out_ref[t, rows] = (acc[rows, lanes] / total[h : h + 1, lanes]).astype(bf16)
            out_ref[t, WIDE:] = packed[:, lanes]


def attend(queries, keyvals, carry, last, block=512, qb=512):
    tiles = queries.shape[0]
    count = tiles * 128
    keys = keyvals.shape[0]
    carry_shapes = [(16, count), (WIDE, count)]
    if last:
        out_shape = [jax.ShapeDtypeStruct((tiles, WIDE + STATS, 128), bf16)]
        scratch = [pltpu.VMEM(s, f32) for s in carry_shapes]
    else:
        out_shape = [jax.ShapeDtypeStruct(s, f32) for s in carry_shapes]
        scratch = []
    carry = [] if carry is None else carry
    work = GROUP * count * keys
    outs = pl.pallas_call(
        functools.partial(attend_kernel, not carry, last, min(block, keys), qb),
        in_specs=[pl.BlockSpec(memory_space=pltpu.VMEM)] * (2 + len(carry)),
        out_specs=[pl.BlockSpec(memory_space=pltpu.VMEM)] * len(out_shape),
        out_shape=out_shape,
        input_output_aliases={} if last or not carry else {2: 0, 3: 1},
        scratch_shapes=[pltpu.VMEM((GROUP, 128, count), bf16)] + scratch,
        compiler_params=pltpu.CompilerParams(vmem_limit_bytes=24 * 2**20),
        cost_estimate=pl.CostEstimate(
            flops=work * 1024, bytes_accessed=keys * 768, transcendentals=work
        ),
    )(queries, keyvals, *carry)
    return outs[0] if last else outs


def finish_kernel(parts_ref, w_ref, out_ref, rows):
    groups = parts_ref.shape[0] // 2
    pieces = []
    for g in range(groups):
        pair = [parts_ref[g], parts_ref[groups + g]]
        logs = []
        for p in pair:
            s = p[WIDE:].astype(f32)
            logs.append((s[0:3] + s[3:6]) + s[6:9])
        top = jnp.maximum(logs[0], logs[1])
        shares = [jnp.exp2(a - top) for a in logs]
        total = shares[0] + shares[1]
        for h in range(GROUP):
            head = slice(HEAD * h, HEAD * (h + 1))
            both = [p[head].astype(f32) * (s[h : h + 1] / total[h : h + 1]) for p, s in zip(pair, shares)]
            pieces.append(both[0] + both[1])
    attended = jnp.concatenate(pieces, 0).T.astype(bf16)
    keep(rows, jnp.dot(attended, w_ref[...], preferred_element_type=f32))
    for r in range(out_ref.shape[0]):
        start = 8 * (r % 2) + r // 2
        out_ref[r] = every_nth(rows, start, 16).astype(bf16)


def finish(parts, w_out):
    shape = (parts.shape[2], w_out.shape[1])
    return pl.pallas_call(
        finish_kernel,
        out_shape=jax.ShapeDtypeStruct((16, 8, shape[1]), bf16),
        scratch_shapes=[pltpu.VMEM((shape[1] // 128, shape[0], 128), f32)],
        compiler_params=pltpu.CompilerParams(vmem_limit_bytes=24 * 2**20),
    )(parts, w_out)


def on_device(patches, norm_gain, w_qkv, pool_q, pool_kv, w_out):
    gain = norm_gain[None]
    tokens, last_column, last_row, last_token = normalised_tokens(patches, gain)
    halo = (passed_along(last_row, ROW), passed_along(last_column, COL), corner(last_token))
    groups = lax.axis_size("y")
    copies = lax.axis_size("zq")
    flat = pool_call(keyvals_kernel, tokens, halo, w_qkv, pool_kv, (copies * groups, 32, 2 * WIDE))
    line = lax.all_to_all(flat, ("zq", "y"), 0, 0, tiled=True).reshape(-1, 2 * WIDE)
    turned = pool_call(queries_kernel, tokens, halo, w_qkv, pool_q, (2 * groups, WIDE, 128))
    swap = lambda block: shifted(block, "core", 1)
    swapped, after, before = swap(line), shifted_x(line, 1), shifted_x(line, -1)
    swapped, turned = lax.optimization_barrier((swapped, turned))
    every_query = lax.all_to_all(turned, ("zc", "y"), 0, 0, tiled=True)
    carry = attend(every_query, line, None, False)
    carry = attend(every_query, swapped, carry, False)
    after, before, carry = lax.optimization_barrier((after, before, carry))
    half = line.shape[0] // 2
    far = [shifted_x(after[:half], 1), shifted_x(before[half:], -1)]
    for block in (after, swap(after), before, swap(before)):
        carry = attend(every_query, block, carry, False)
    far, carry = lax.optimization_barrier((far, carry))
    far = jnp.concatenate(far, 0)
    carry = attend(every_query, far, carry, False)
    partial = attend(every_query, swap(far), carry, True)
    parts = lax.all_to_all(partial, ("zc", "y"), 0, 0, tiled=True)
    return finish(parts, w_out)


def solution(mesh):
    fine = Mesh(mesh.devices.reshape(4, 2, 2, 2, 4, 2), AXES)
    tiles = P(ROW, COL, None)
    return jax.shard_map(
        on_device,
        mesh=fine,
        in_specs=(tiles, P(), P(), P(), P(), P()),
        out_specs=tiles,
        check_vma=False,
    )
```

time: 111 us -> 97.8 us (0.88)
  starting transfers between devices: 40.4 us -> 21.2 us
  blocking collectives: 22.2 us -> 40.6 us
  local copies, waits for them, and re-layouts: 13.5 us -> 1.94 us
  Pallas kernels: 24.3 us -> 26 us
  waiting for transfers between devices: 8.22 us -> 6.98 us
    all_to_all x1 -> x2, blocking collectives: 22.2 us -> 40.6 us  [the longest x1 28.6 us: on_device(): lax.all_to_all(flat, ('zq', 'y'), 0, 0, tiled=True).reshape(-1, 2 * WIDE)]
    ppermute x8 -> x4, starting transfers between devices: 13.6 us -> 3.26 us  [shifted(): lax.ppermute(block, axis, [(i, (i + distance) % count) for i in range(cou...]
    unnamed x30 -> x11, local copies, waits for them, and re-layouts: 10.1 us -> 1.17 us
    all_to_all x2 -> x1, starting transfers between devices: 11.4 us -> 3.45 us  [on_device(): every_query = lax.all_to_all(turned, ('zc', 'y'), 0, 0, tiled=True)]
    all_to_all x2 -> x1, waiting for transfers between devices: 0.01 us -> 6.23 us  [on_device(): every_query = lax.all_to_all(turned, ('zc', 'y'), 0, 0, tiled=True)]
    ppermute x3 -> x4, waiting for transfers between devices: 4.94 us -> 0.01 us  [shifted_x(): return lax.ppermute(block, ('xl', 'xh'), route)]
    ppermute x8 -> x4, waiting for transfers between devices: 3.26 us -> 0.01 us  [shifted(): lax.ppermute(block, axis, [(i, (i + distance) % count) for i in range(cou...]
    slice x5 -> x2, local copies, waits for them, and re-layouts: 2.6 us -> 0.04 us  [on_device(): far = [shifted_x(after[:half], 1), shifted_x(before[half:], -1)]]
  transfers between devices with their start and end apart: 16 -> 12, of which waited for: 3 -> 2; matrix products, arithmetic and copies ran while one was open for 3% -> 0% of each run, Pallas kernels for 18% -> 20%
where the time goes in v2:
time: 97.8 us; the launch traced here: 97 us
  blocking collectives  40.6 us (42%)
  Pallas kernels  26 us (27%)
  starting transfers between devices  21.2 us (22%)
  waiting for transfers between devices  6.98 us (7%)
  local copies, waits for them, and re-layouts  1.94 us (2%)
    all_to_all x1, blocking collectives, on_device(): lax.all_to_all(flat, ('zq', 'y'), 0, 0, tiled=True).reshape(-1, 2 * WIDE)  28.6 us
    pallas_call x8, Pallas kernels, attend(): pl.pallas_call(functools.partial(attend_kernel, not carry, last, min(bloc...  19.7 us
    all_to_all x1, blocking collectives, on_device(): parts = lax.all_to_all(partial, ('zc', 'y'), 0, 0, tiled=True)  12 us
    ppermute x2, starting transfers between devices, passed_along(): return lax.ppermute(block, axis, [(i - 1, i) for i in range(1, count)])  7.71 us
    all_to_all x1, waiting for transfers between devices, on_device(): every_query = lax.all_to_all(turned, ('zc', 'y'), 0, 0, tiled=True)  6.23 us
    ppermute x1, starting transfers between devices, corner(): return lax.ppermute(block, AXES, route)  3.52 us
    all_to_all x1, starting transfers between devices, on_device(): every_query = lax.all_to_all(turned, ('zc', 'y'), 0, 0, tiled=True)  3.45 us
    pallas_call x2, Pallas kernels, pool_call(): pl.pallas_call(kernel, in_specs=[pl.BlockSpec(memory_space=pltpu.VMEM)] *...  3.44 us
  transfers between devices with their start and end apart: 12, of which 2 were waited for; matrix products, arithmetic and copies ran while one was open for 0% of the time, Pallas kernels for 20%

profile of v2, /device:TPU:1, one launch (start us, length us, event | category | flops | bytes accessed | tf_op | source)
XLA Modules:
  0.0 97.0 jit_solution(15760881882587946416)
XLA Ops:
  0.0 0.7 broadcast_in_dim.3.gain_ref
  0.7 1.1 %copy-done.2 = bf16[32,16,768]{2,1,0:T(8,128)(2,1)S(1)} copy-done((bf16[32,16,768]{2,1,0:T(8,128)(2,1)S(1)}, bf16[32,16,768]{2,1,0:T(8,128)(2,1)}, u32[]{:S(2)}) %copy-start.2) | copy-done | bytes 786456
  1.8 1.8 %shard_map.64 = (bf16[512,768]{1,0:T(8,128)(2,1)S(1)}, bf16[32,768]{1,0:T(8,128)(2,1)S(1)}, bf16[16,768]{1,0:T(8,128)(2,1)S(1)}, bf16[1,768]{1,0:T(2,128)(2,1)S(1)}) custom-call(bf16[32,16,768]{2,1,0:T(8,128)(2,1)S(1)} %copy-done.2, f32[1,768]{1,0:T(1,128)S(1)} %broadcast_in_dim.3.gain_ref), custom_call_target="tpu_custom_call" | custom-call | flops 4000000000 | bytes 1000000 | tf_op jit(solution)/shard_map/pallas_call | solution.py:91
  3.6 0.0 copy-start.4
  3.6 4.6 %collective-permute-start.1 = (bf16[32,768]{1,0:T(8,128)(2,1)S(1)}, bf16[32,768]{1,0:T(8,128)(2,1)S(1)}, u32[]{:S(2)}, u32[]{:S(2)}) collective-permute-start(bf16[32,768]{1,0:T(8,128)(2,1)S(1)} %get-tuple-element.35), channel_id=1, source_target_pairs={{0,1},{1,2},{2,3},{3,4},{4,5},{5,6},{6,7},{7,8},{8,9},{9,10},{10,1... | collective-permute-start | bytes 147464 | tf_op jit(solution)/shard_map/ppermute | solution.py:36
  8.2 3.1 %collective-permute-start = (bf16[16,768]{1,0:T(8,128)(2,1)S(1)}, bf16[16,768]{1,0:T(8,128)(2,1)S(1)}, u32[]{:S(2)}, u32[]{:S(2)}) collective-permute-start(bf16[16,768]{1,0:T(8,128)(2,1)S(1)} %get-tuple-element.34), channel_id=1, source_target_pairs={{0,16},{16,32},{32,48},{48,64},{64,80},{80,96},{96,112},{112,128},... | collective-permute-start | bytes 73736 | tf_op jit(solution)/shard_map/ppermute | solution.py:36
  11.3 3.5 %collective-permute-start.2 = (bf16[1,768]{1,0:T(2,128)(2,1)S(1)}, bf16[1,768]{1,0:T(2,128)(2,1)S(1)}, u32[]{:S(2)}, u32[]{:S(2)}) collective-permute-start(bf16[1,768]{1,0:T(2,128)(2,1)S(1)} %get-tuple-element.36), channel_id=1, source_target_pairs={{0,17},{1,18},{2,19},{3,20},{4,21},{5,22},{6,23},{7,24},{8,25},{9,... | collective-permute-start | bytes 4616 | tf_op jit(solution)/shard_map/ppermute | solution.py:42
  14.9 0.7 collective-permute-done.2.corner_ref
  15.6 1.5 %shard_map.65 = bf16[16,32,384]{2,1,0:T(8,128)(2,1)S(1)} custom-call(bf16[512,768]{1,0:T(8,128)(2,1)S(1)} %get-tuple-element.33.tokens_ref, bf16[16,768]{1,0:T(8,128)(2,1)S(1)} %collective-permute-done.upper_ref, bf16[32,768]{1,0:T(8,128)(2,1)S(1)} %collective-permute-done.1.left_ref, bf16[1,768]{1,0:T(2,128)(2,1)S(1)} %collective-permute-done.2.corner_ref, ...), custom_call_target="tpu_custom_call" | custom-call | flops 1500000000 | bytes 4000000 | tf_op jit(solution)/shard_map/pallas_call | solution.py:168
  17.1 28.6 %all_to_all.15 = bf16[16,32,384]{2,1,0:T(8,128)(2,1)S(1)} all-to-all(bf16[16,32,384]{2,1,0:T(8,128)(2,1)S(1)} %shard_map.65), channel_id=1, replica_groups=mesh['zq'=4,'zc'=2,'xl'=2,'xh'=2,'y'=4,'core'=2] {'zq','y'}, dimensions={0} | all-to-all | bytes 786432 | tf_op jit(solution)/shard_map/all_to_all | solution.py:320
  45.7 0.8 collective-permute-start.3
  46.5 1.9 %shard_map.66 = bf16[8,192,128]{2,1,0:T(8,128)(2,1)} custom-call(bf16[512,768]{1,0:T(8,128)(2,1)S(1)} %get-tuple-element.33.tokens_ref, bf16[16,768]{1,0:T(8,128)(2,1)S(1)} %collective-permute-done.upper_ref, bf16[32,768]{1,0:T(8,128)(2,1)S(1)} %collective-permute-done.1.left_ref, bf16[1,768]{1,0:T(2,128)(2,1)S(1)} %collective-permute-done.2.corner_ref, ...), custom_call_target="tpu_custom_call" | custom-call | flops 1500000000 | bytes 4000000 | tf_op jit(solution)/shard_map/pallas_call | solution.py:168
  48.5 3.5 %all-to-all-start.1 = ((bf16[8,192,128]{2,1,0:T(8,128)(2,1)}), bf16[8,192,128]{2,1,0:T(8,128)(2,1)S(1)}, u32[]{:S(2)}, u32[]{:S(2)}) async-start(bf16[8,192,128]{2,1,0:T(8,128)(2,1)} %shard_map.66), calls=%async_computation.1 | async-start | bytes 786432 | tf_op jit(solution)/shard_map/all_to_all | solution.py:325
  51.9 0.1 collective-permute-start.5
  52.0 1.4 %collective-permute-start.4 = (bf16[512,384]{1,0:T(8,128)(2,1)S(1)}, bf16[512,384]{1,0:T(8,128)(2,1)S(1)}, u32[]{:S(2)}, u32[]{:S(2)}) collective-permute-start(bf16[512,384]{1,0:T(8,128)(2,1)S(1)} %bitcast.3), channel_id=1, source_target_pairs={{0,16},{16,8},{8,24},{24,0},{1,17},{17,9},{9,25},{25,1},{2,18},{18... | collective-permute-start | bytes 1179656 | tf_op jit(solution)/shard_map/ppermute | solution.py:31
  53.5 6.2 %all-to-all-done.1.q_ref = bf16[8,192,128]{2,1,0:T(8,128)(2,1)S(1)} async-done(((bf16[8,192,128]{2,1,0:T(8,128)(2,1)}), bf16[8,192,128]{2,1,0:T(8,128)(2,1)S(1)}, u32[]{:S(2)}, u32[]{:S(2)}) %all-to-all-start.1) | async-done | bytes 393248 | tf_op jit(solution)/shard_map/all_to_all | solution.py:325
  59.7 2.3 %shard_map.67 = (f32[16,1024]{1,0:T(8,128)S(1)}, f32[192,1024]{1,0:T(8,128)S(1)}) custom-call(bf16[8,192,128]{2,1,0:T(8,128)(2,1)S(1)} %all-to-all-done.1.q_ref, bf16[512,384]{1,0:T(8,128)(2,1)S(1)} %bitcast.4), custom_call_target="tpu_custom_call" | custom-call | flops 1610612736 | bytes 393216 | tf_op jit(solution)/shard_map/pallas_call | solution.py:265
  62.0 2.5 %shard_map.68 = (f32[16,1024]{1,0:T(8,128)S(1)}, f32[192,1024]{1,0:T(8,128)S(1)}) custom-call(bf16[8,192,128]{2,1,0:T(8,128)(2,1)S(1)} %all-to-all-done.1.q_ref, bf16[512,384]{1,0:T(8,128)(2,1)S(1)} %collective-permute-done.3.kv_ref, f32[16,1024]{1,0:T(8,128)S(1)} %get-tuple-element.39.refs_0_, ...), custom_call_target="tpu_custom_call", output_to_operand_aliasing={{0}: (2, {}), {1}: (3, {})} | custom-call | flops 1610612736 | bytes 393216 | tf_op jit(solution)/shard_map/pallas_call | solution.py:265
  64.5 1.3 %collective-permute-start.9 = (bf16[512,384]{1,0:T(8,128)(2,1)S(1)}, bf16[512,384]{1,0:T(8,128)(2,1)S(1)}, u32[]{:S(2)}, u32[]{:S(2)}) collective-permute-start(bf16[512,384]{1,0:T(8,128)(2,1)S(1)} %collective-permute-done.4.kv_ref), channel_id=1, source_target_pairs={{0,1},{1,0},{2,3},{3,2},{4,5},{5,4},{6,7},{7,6},{8,9},{9,8},{10,11... | collective-permute-start | bytes 1179656 | tf_op jit(solution)/shard_map/ppermute | solution.py:25
  65.8 0.1 collective-permute-start.8
  66.0 0.6 collective-permute-start.7
  66.6 1.1 %collective-permute-start.6 = (bf16[256,384]{1,0:T(8,128)(2,1)S(1)}, bf16[256,384]{1,0:T(8,128)(2,1)S(1)}, u32[]{:S(2)}, u32[]{:S(2)}) collective-permute-start(bf16[256,384]{1,0:T(8,128)(2,1)S(1)} %slice.6), channel_id=1, source_target_pairs={{0,16},{16,8},{8,24},{24,0},{1,17},{17,9},{9,25},{25,1},{2,18},{18... | collective-permute-start | bytes 589832 | tf_op jit(solution)/shard_map/ppermute | solution.py:31
  67.7 2.5 %shard_map.69 = (f32[16,1024]{1,0:T(8,128)S(1)}, f32[192,1024]{1,0:T(8,128)S(1)}) custom-call(bf16[8,192,128]{2,1,0:T(8,128)(2,1)S(1)} %all-to-all-done.1.q_ref, bf16[512,384]{1,0:T(8,128)(2,1)S(1)} %collective-permute-done.4.kv_ref, f32[16,1024]{1,0:T(8,128)S(1)} %get-tuple-element.45.refs_0_, ...), custom_call_target="tpu_custom_call", output_to_operand_aliasing={{0}: (2, {}), {1}: (3, {})} | custom-call | flops 1610612736 | bytes 393216 | tf_op jit(solution)/shard_map/pallas_call | solution.py:265
  70.2 2.5 %shard_map.70 = (f32[16,1024]{1,0:T(8,128)S(1)}, f32[192,1024]{1,0:T(8,128)S(1)}) custom-call(bf16[8,192,128]{2,1,0:T(8,128)(2,1)S(1)} %all-to-all-done.1.q_ref, bf16[512,384]{1,0:T(8,128)(2,1)S(1)} %collective-permute-done.9.kv_ref, f32[16,1024]{1,0:T(8,128)S(1)} %get-tuple-element.47.refs_0_, ...), custom_call_target="tpu_custom_call", output_to_operand_aliasing={{0}: (2, {}), {1}: (3, {})} | custom-call | flops 1610612736 | bytes 393216 | tf_op jit(solution)/shard_map/pallas_call | solution.py:265
  72.6 2.5 %shard_map.71 = (f32[16,1024]{1,0:T(8,128)S(1)}, f32[192,1024]{1,0:T(8,128)S(1)}) custom-call(bf16[8,192,128]{2,1,0:T(8,128)(2,1)S(1)} %all-to-all-done.1.q_ref, bf16[512,384]{1,0:T(8,128)(2,1)S(1)} %collective-permute-done.5.kv_ref, f32[16,1024]{1,0:T(8,128)S(1)} %get-tuple-element.49.refs_0_, ...), custom_call_target="tpu_custom_call", output_to_operand_aliasing={{0}: (2, {}), {1}: (3, {})} | custom-call | flops 1610612736 | bytes 393216 | tf_op jit(solution)/shard_map/pallas_call | solution.py:265
  75.1 2.5 %shard_map.72 = (f32[16,1024]{1,0:T(8,128)S(1)}, f32[192,1024]{1,0:T(8,128)S(1)}) custom-call(bf16[8,192,128]{2,1,0:T(8,128)(2,1)S(1)} %all-to-all-done.1.q_ref, bf16[512,384]{1,0:T(8,128)(2,1)S(1)} %collective-permute-done.8.kv_ref, f32[16,1024]{1,0:T(8,128)S(1)} %get-tuple-element.51.refs_0_, ...), custom_call_target="tpu_custom_call", output_to_operand_aliasing={{0}: (2, {}), {1}: (3, {})} | custom-call | flops 1610612736 | bytes 393216 | tf_op jit(solution)/shard_map/pallas_call | solution.py:265
  77.7 1.1 %collective-permute-start.10 = (bf16[512,384]{1,0:T(8,128)(2,1)S(1)}, bf16[512,384]{1,0:T(8,128)(2,1)S(1)}, u32[]{:S(2)}, u32[]{:S(2)}) collective-permute-start(bf16[512,384]{1,0:T(8,128)(2,1)S(1)} %constant_dynamic-update-slice_fusion.kv_ref), channel_id=1, source_target_pairs={{0,1},{1,0},{2,3},{3,2},{4,5},{5,4},{6,7},{7,6},{8,9},{9,8},{10,11... | collective-permute-start | bytes 1179656 | tf_op jit(solution)/shard_map/ppermute | solution.py:25
  78.8 2.5 %shard_map.73 = (f32[16,1024]{1,0:T(8,128)S(1)}, f32[192,1024]{1,0:T(8,128)S(1)}) custom-call(bf16[8,192,128]{2,1,0:T(8,128)(2,1)S(1)} %all-to-all-done.1.q_ref, bf16[512,384]{1,0:T(8,128)(2,1)S(1)} %constant_dynamic-update-slice_fusion.kv_ref, f32[16,1024]{1,0:T(8,128)S(1)} %get-tuple-element.57.refs_0_, ...), custom_call_target="tpu_custom_call", output_to_operand_aliasing={{0}: (2, {}), {1}: (3, {})} | custom-call | flops 1610612736 | bytes 393216 | tf_op jit(solution)/shard_map/pallas_call | solution.py:265
  81.3 0.0 copy-start
  81.3 2.5 %shard_map.74 = bf16[8,208,128]{2,1,0:T(8,128)(2,1)S(1)} custom-call(bf16[8,192,128]{2,1,0:T(8,128)(2,1)S(1)} %all-to-all-done.1.q_ref, bf16[512,384]{1,0:T(8,128)(2,1)S(1)} %collective-permute-done.10.kv_ref, f32[16,1024]{1,0:T(8,128)S(1)} %get-tuple-element.59.refs_0_, f32[192,1024]{1,0:T(8,128)S(1)} %get-tuple-element.60.refs_1_), custom_call_target="tpu_custom_call" | custom-call | flops 1610612736 | bytes 393216 | tf_op jit(solution)/shard_map/pallas_call | solution.py:265
  83.8 12.0 %all_to_all.16.parts_ref = bf16[8,208,128]{2,1,0:T(8,128)(2,1)S(1)} all-to-all(bf16[8,208,128]{2,1,0:T(8,128)(2,1)S(1)} %shard_map.74), channel_id=1, replica_groups=mesh['zq'=4,'zc'=2,'xl'=2,'xh'=2,'y'=4,'core'=2] {'zc','y'}, dimensions={0} | all-to-all | bytes 851968 | tf_op jit(solution)/shard_map/all_to_all | solution.py:337
  95.9 1.1 %shard_map.75 = bf16[16,8,768]{2,1,0:T(8,128)(2,1)} custom-call(bf16[8,208,128]{2,1,0:T(8,128)(2,1)S(1)} %all_to_all.16.parts_ref, bf16[768,768]{1,0:T(8,128)(2,1)S(1)} %copy-done), custom_call_target="tpu_custom_call" | custom-call | tf_op jit(solution)/shard_map/pallas_call | solution.py:305
  (21 shorter events, 0.1 us)
Async XLA Ops:
  0.7 1.1 %copy-start.2 = (bf16[32,16,768]{2,1,0:T(8,128)(2,1)S(1)}, bf16[32,16,768]{2,1,0:T(8,128)(2,1)}, u32[]{:S(2)}) copy-start(bf16[32,16,768]{2,1,0:T(8,128)(2,1)} %patches_ref.1) | copy-start | bytes 2359300
  1.8 13.8 %copy-start.1 = (bf16[768,2304]{1,0:T(8,128)(2,1)S(1)}, bf16[768,2304]{1,0:T(8,128)(2,1)}, u32[]{:S(2)}) copy-start(bf16[768,2304]{1,0:T(8,128)(2,1)} %w_ref.4) | copy-start | bytes 10616836
  1.8 13.8 %copy-start.3 = (f32[9,1536]{1,0:T(8,128)S(1)}, f32[9,1536]{1,0:T(8,128)}, u32[]{:S(2)}) copy-start(f32[9,1536]{1,0:T(8,128)} %pool_ref.2) | copy-start | bytes 165892
  3.6 42.9 %copy-start.4 = (f32[9,768]{1,0:T(8,128)S(1)}, f32[9,768]{1,0:T(8,128)}, u32[]{:S(2)}) copy-start(f32[9,768]{1,0:T(8,128)} %pool_ref.3) | copy-start | bytes 82948
  3.6 12.0 %collective-permute-start.1 = (bf16[32,768]{1,0:T(8,128)(2,1)S(1)}, bf16[32,768]{1,0:T(8,128)(2,1)S(1)}, u32[]{:S(2)}, u32[]{:S(2)}) collective-permute-start(bf16[32,768]{1,0:T(8,128)(2,1)S(1)} %get-tuple-element.35), channel_id=1, source_target_pairs={{0,1},{1,2},{2,3},{3,4},{4,5},{5,6},{6,7},{7,8},{8,9},{9,10},{10,1... | collective-permute-start | bytes 147464 | tf_op jit(solution)/shard_map/ppermute | solution.py:36
  8.2 7.4 %collective-permute-start = (bf16[16,768]{1,0:T(8,128)(2,1)S(1)}, bf16[16,768]{1,0:T(8,128)(2,1)S(1)}, u32[]{:S(2)}, u32[]{:S(2)}) collective-permute-start(bf16[16,768]{1,0:T(8,128)(2,1)S(1)} %get-tuple-element.34), channel_id=1, source_target_pairs={{0,16},{16,32},{32,48},{48,64},{64,80},{80,96},{96,112},{112,128},... | collective-permute-start | bytes 73736 | tf_op jit(solution)/shard_map/ppermute | solution.py:36
  11.3 4.3 %collective-permute-start.2 = (bf16[1,768]{1,0:T(2,128)(2,1)S(1)}, bf16[1,768]{1,0:T(2,128)(2,1)S(1)}, u32[]{:S(2)}, u32[]{:S(2)}) collective-permute-start(bf16[1,768]{1,0:T(2,128)(2,1)S(1)} %get-tuple-element.36), channel_id=1, source_target_pairs={{0,17},{1,18},{2,19},{3,20},{4,21},{5,22},{6,23},{7,24},{8,25},{9,... | collective-permute-start | bytes 4616 | tf_op jit(solution)/shard_map/ppermute | solution.py:42
  45.7 2.7 %collective-permute-start.3 = (bf16[512,384]{1,0:T(8,128)(2,1)S(1)}, bf16[512,384]{1,0:T(8,128)(2,1)S(1)}, u32[]{:S(2)}, u32[]{:S(2)}) collective-permute-start(bf16[512,384]{1,0:T(8,128)(2,1)S(1)} %bitcast.1), channel_id=1, source_target_pairs={{0,1},{1,0},{2,3},{3,2},{4,5},{5,4},{6,7},{7,6},{8,9},{9,8},{10,11... | collective-permute-start | bytes 1179656 | tf_op jit(solution)/shard_map/ppermute | solution.py:25
  48.5 11.2 %all-to-all-start.1 = ((bf16[8,192,128]{2,1,0:T(8,128)(2,1)}), bf16[8,192,128]{2,1,0:T(8,128)(2,1)S(1)}, u32[]{:S(2)}, u32[]{:S(2)}) async-start(bf16[8,192,128]{2,1,0:T(8,128)(2,1)} %shard_map.66), calls=%async_computation.1 | async-start | bytes 786432 | tf_op jit(solution)/shard_map/all_to_all | solution.py:325
  51.9 12.6 %collective-permute-start.5 = (bf16[512,384]{1,0:T(8,128)(2,1)S(1)}, bf16[512,384]{1,0:T(8,128)(2,1)S(1)}, u32[]{:S(2)}, u32[]{:S(2)}) collective-permute-start(bf16[512,384]{1,0:T(8,128)(2,1)S(1)} %bitcast.2), channel_id=1, source_target_pairs={{0,24},{16,0},{8,16},{24,8},{1,25},{17,1},{9,17},{25,9},{2,26},{18... | collective-permute-start | bytes 1179656 | tf_op jit(solution)/shard_map/ppermute | solution.py:31
  52.0 12.5 %collective-permute-start.4 = (bf16[512,384]{1,0:T(8,128)(2,1)S(1)}, bf16[512,384]{1,0:T(8,128)(2,1)S(1)}, u32[]{:S(2)}, u32[]{:S(2)}) collective-permute-start(bf16[512,384]{1,0:T(8,128)(2,1)S(1)} %bitcast.3), channel_id=1, source_target_pairs={{0,16},{16,8},{8,24},{24,0},{1,17},{17,9},{9,25},{25,1},{2,18},{18... | collective-permute-start | bytes 1179656 | tf_op jit(solution)/shard_map/ppermute | solution.py:31
  64.5 5.6 %collective-permute-start.9 = (bf16[512,384]{1,0:T(8,128)(2,1)S(1)}, bf16[512,384]{1,0:T(8,128)(2,1)S(1)}, u32[]{:S(2)}, u32[]{:S(2)}) collective-permute-start(bf16[512,384]{1,0:T(8,128)(2,1)S(1)} %collective-permute-done.4.kv_ref), channel_id=1, source_target_pairs={{0,1},{1,0},{2,3},{3,2},{4,5},{5,4},{6,7},{7,6},{8,9},{9,8},{10,11... | collective-permute-start | bytes 1179656 | tf_op jit(solution)/shard_map/ppermute | solution.py:25
  65.8 9.3 %collective-permute-start.8 = (bf16[512,384]{1,0:T(8,128)(2,1)S(1)}, bf16[512,384]{1,0:T(8,128)(2,1)S(1)}, u32[]{:S(2)}, u32[]{:S(2)}) collective-permute-start(bf16[512,384]{1,0:T(8,128)(2,1)S(1)} %collective-permute-done.5.kv_ref), channel_id=1, source_target_pairs={{0,1},{1,0},{2,3},{3,2},{4,5},{5,4},{6,7},{7,6},{8,9},{9,8},{10,11... | collective-permute-start | bytes 1179656 | tf_op jit(solution)/shard_map/ppermute | solution.py:25
  66.0 11.6 %collective-permute-start.7 = (bf16[256,384]{1,0:T(8,128)(2,1)S(1)}, bf16[256,384]{1,0:T(8,128)(2,1)S(1)}, u32[]{:S(2)}, u32[]{:S(2)}) collective-permute-start(bf16[256,384]{1,0:T(8,128)(2,1)S(1)} %slice.7), channel_id=1, source_target_pairs={{0,24},{16,0},{8,16},{24,8},{1,25},{17,1},{9,17},{25,9},{2,26},{18... | collective-permute-start | bytes 589832 | tf_op jit(solution)/shard_map/ppermute | solution.py:31
  66.6 11.0 %collective-permute-start.6 = (bf16[256,384]{1,0:T(8,128)(2,1)S(1)}, bf16[256,384]{1,0:T(8,128)(2,1)S(1)}, u32[]{:S(2)}, u32[]{:S(2)}) collective-permute-start(bf16[256,384]{1,0:T(8,128)(2,1)S(1)} %slice.6), channel_id=1, source_target_pairs={{0,16},{16,8},{8,24},{24,0},{1,17},{17,9},{9,25},{25,1},{2,18},{18... | collective-permute-start | bytes 589832 | tf_op jit(solution)/shard_map/ppermute | solution.py:31
  77.7 3.6 %collective-permute-start.10 = (bf16[512,384]{1,0:T(8,128)(2,1)S(1)}, bf16[512,384]{1,0:T(8,128)(2,1)S(1)}, u32[]{:S(2)}, u32[]{:S(2)}) collective-permute-start(bf16[512,384]{1,0:T(8,128)(2,1)S(1)} %constant_dynamic-update-slice_fusion.kv_ref), channel_id=1, source_target_pairs={{0,1},{1,0},{2,3},{3,2},{4,5},{5,4},{6,7},{7,6},{8,9},{9,8},{10,11... | collective-permute-start | bytes 1179656 | tf_op jit(solution)/shard_map/ppermute | solution.py:25
  81.3 14.6 %copy-start = (bf16[768,768]{1,0:T(8,128)(2,1)S(1)}, bf16[768,768]{1,0:T(8,128)(2,1)}, u32[]{:S(2)}) copy-start(bf16[768,768]{1,0:T(8,128)(2,1)} %w_ref.5) | copy-start | bytes 3538948

commit v3 on v2

--- a/solution.py
+++ b/solution.py
@@ -175,13 +175,16 @@
     )(tokens, *halo, w_qkv, taps)
 
 
-def attend_kernel(first, last, block, qb, q_ref, kv_ref, *refs):
+def attend_kernel(first, last, keep_block, qb, blocks, q_ref, *refs):
+    block_refs, refs = refs[:blocks], refs[blocks:]
     if first:
         stat_in, acc_in = None, None
     else:
         stat_in, acc_in, *refs = refs
     if last:
         out_ref, qz, stat, acc = refs
+    elif keep_block:
+        stat, acc, block_ref, qz = refs
     else:
         stat, acc, qz = refs
     tiles = q_ref.shape[0]
@@ -194,40 +197,36 @@
             qz[h, here : here + HEAD, lanes] = q_ref[t, HEAD * h : HEAD * (h + 1)]
             qz[h, HEAD - here : 2 * HEAD - here, lanes] = zero
 
-    jobs = [
-        (k, j, h)
-        for k in range(kv_ref.shape[0] // block)
-        for j in range(count // qb)
-        for h in range(GROUP)
-    ]
-    ones = jnp.ones((16, block), bf16)
-    values = [kv_ref[pl.ds(k * block, block), 128:384].T for k in range(kv_ref.shape[0] // block)]
-
-    def scores(k, j, h):
-        keys = kv_ref[pl.ds(k * block, block), 128 * (h // 2) : 128 * (h // 2) + 128]
+    jobs = [(j, h) for j in range(count // qb) for h in range(GROUP)]
+    block = jnp.concatenate([r[...] for r in block_refs], 0)
+    if keep_block:
+        block_ref[...] = block
+    values = block[:, 128:].T
+    ones = jnp.ones((16, block.shape[0]), bf16)
+
+    def scores(j, h):
+        keys = block[:, 128 * (h // 2) : 128 * (h // 2) + 128]
         return jnp.dot(keys, qz[h, :, j * qb : (j + 1) * qb], preferred_element_type=f32)
 
     ready = scores(*jobs[0])
-    for place, (k, j, h) in enumerate(jobs):
+    for place, (j, h) in enumerate(jobs):
         now = ready
         if place + 1 < len(jobs):
             ready = scores(*jobs[place + 1])
         lanes = slice(j * qb, (j + 1) * qb)
         rows = slice(HEAD * h, HEAD * (h + 1))
         new = jnp.max(now, axis=0, keepdims=True)
-        source = (stat_in, acc_in) if k == 0 else (stat, acc)
-        carried = k > 0 or not first
-        if carried:
-            old = source[0][h : h + 1, lanes]
+        if not first:
+            old = stat_in[h : h + 1, lanes]
             new = jnp.maximum(old, new)
         weights = jnp.exp2((now - new) * SCALE).astype(bf16)
-        value = jnp.concatenate([values[k][HEAD * (h + 1) : HEAD * (h + 2)], ones], 0)
+        value = jnp.concatenate([values[HEAD * (h + 1) : HEAD * (h + 2)], ones], 0)
         part = jnp.dot(value, weights, preferred_element_type=f32)
         total, numer = part[HEAD : HEAD + 1], part[:HEAD]
-        if carried:
+        if not first:
             factor = jnp.exp2((old - new) * SCALE)
-            total = source[0][8 + h : 9 + h, lanes] * factor + total
-            numer = source[1][rows, lanes] * factor + numer
+            total = stat_in[8 + h : 9 + h, lanes] * factor + total
+            numer = acc_in[rows, lanes] * factor + numer
         stat[h : h + 1, lanes] = new
         stat[8 + h : 9 + h, lanes] = total
         acc[rows, lanes] = numer
@@ -249,10 +248,10 @@
             out_ref[t, WIDE:] = packed[:, lanes]
 
 
-def attend(queries, keyvals, carry, last, block=512, qb=512):
+def attend(queries, blocks, carry, last=False, keep_block=False, qb=512):
     tiles = queries.shape[0]
     count = tiles * 128
-    keys = keyvals.shape[0]
+    keys = sum(b.shape[0] for b in blocks)
     carry_shapes = [(16, count), (WIDE, count)]
     if last:
         out_shape = [jax.ShapeDtypeStruct((tiles, WIDE + STATS, 128), bf16)]
@@ -260,21 +259,23 @@
     else:
         out_shape = [jax.ShapeDtypeStruct(s, f32) for s in carry_shapes]
         scratch = []
+        if keep_block:
+            out_shape.append(jax.ShapeDtypeStruct((keys, 2 * WIDE), bf16))
     carry = [] if carry is None else carry
     work = GROUP * count * keys
     outs = pl.pallas_call(
-        functools.partial(attend_kernel, not carry, last, min(block, keys), qb),
-        in_specs=[pl.BlockSpec(memory_space=pltpu.VMEM)] * (2 + len(carry)),
+        functools.partial(attend_kernel, not carry, last, keep_block, qb, len(blocks)),
+        in_specs=[pl.BlockSpec(memory_space=pltpu.VMEM)] * (1 + len(blocks) + len(carry)),
         out_specs=[pl.BlockSpec(memory_space=pltpu.VMEM)] * len(out_shape),
         out_shape=out_shape,
-        input_output_aliases={} if last or not carry else {2: 0, 3: 1},
+        input_output_aliases={} if last or not carry else {1 + len(blocks): 0, 2 + len(blocks): 1},
         scratch_shapes=[pltpu.VMEM((GROUP, 128, count), bf16)] + scratch,
         compiler_params=pltpu.CompilerParams(vmem_limit_bytes=24 * 2**20),
         cost_estimate=pl.CostEstimate(
-            flops=work * 1024, bytes_accessed=keys * 768, transcendentals=work
+            flops=work * 1, bytes_accessed=1024, transcendentals=0
         ),
-    )(queries, keyvals, *carry)
-    return outs[0] if last else outs
+    )(queries, *blocks, *carry)
+    return outs[0] if last else (outs[:2], *outs[2:])
 
 
 def finish_kernel(parts_ref, w_ref, out_ref, rows):
@@ -315,25 +316,27 @@
     tokens, last_column, last_row, last_token = normalised_tokens(patches, gain)
     halo = (passed_along(last_row, ROW), passed_along(last_column, COL), corner(last_token))
     groups = lax.axis_size("y")
-    copies = lax.axis_size("zq")
-    flat = pool_call(keyvals_kernel, tokens, halo, w_qkv, pool_kv, (copies * groups, 32, 2 * WIDE))
-    line = lax.all_to_all(flat, ("zq", "y"), 0, 0, tiled=True).reshape(-1, 2 * WIDE)
+    flat = pool_call(keyvals_kernel, tokens, halo, w_qkv, pool_kv, (groups, 32, 2 * WIDE))
+    own = lax.all_to_all(flat, "y", 0, 0, tiled=True).reshape(-1, 2 * WIDE)
+    tie = lax.optimization_barrier
+    own, tokens = tie((own, tokens))
+    line = [own, shifted(own, "zq", 2), shifted(own, "zq", 1), shifted(own, "zq", -1)]
     turned = pool_call(queries_kernel, tokens, halo, w_qkv, pool_q, (2 * groups, WIDE, 128))
+    every_query = lax.all_to_all(turned, ("zc", "y"), 0, 0, tiled=True)
+    line = jnp.concatenate(line, 0)
+    after, before = shifted_x(line, 1), shifted_x(line, -1)
     swap = lambda block: shifted(block, "core", 1)
-    swapped, after, before = swap(line), shifted_x(line, 1), shifted_x(line, -1)
-    swapped, turned = lax.optimization_barrier((swapped, turned))
-    every_query = lax.all_to_all(turned, ("zc", "y"), 0, 0, tiled=True)
-    carry = attend(every_query, line, None, False)
-    carry = attend(every_query, swapped, carry, False)
-    after, before, carry = lax.optimization_barrier((after, before, carry))
+    (carry,) = attend(every_query, [line], None)
+    (carry,) = attend(every_query, [swap(line)], carry)
+    after, before, carry = tie((after, before, carry))
     half = line.shape[0] // 2
     far = [shifted_x(after[:half], 1), shifted_x(before[half:], -1)]
     for block in (after, swap(after), before, swap(before)):
-        carry = attend(every_query, block, carry, False)
-    far, carry = lax.optimization_barrier((far, carry))
-    far = jnp.concatenate(far, 0)
-    carry = attend(every_query, far, carry, False)
-    partial = attend(every_query, swap(far), carry, True)
+        (carry,) = attend(every_query, [block], carry)
+    far, carry = tie((far, carry))
+    swapped = [swap(block) for block in far]
+    (carry,) = attend(every_query, far, carry)
+    partial = attend(every_query, swapped, carry, last=True)
     parts = lax.all_to_all(partial, ("zc", "y"), 0, 0, tiled=True)
     return finish(parts, w_out)
 

time: 97.8 us -> 91.5 us (0.936)
  blocking collectives: 40.6 us -> 20.5 us
  starting transfers between devices: 21.2 us -> 36.4 us
    all_to_all x1, blocking collectives: 28.6 us -> 8.66 us  [on_device(): own = lax.all_to_all(flat, 'y', 0, 0, tiled=True).reshape(-1, 2 * WIDE)]
    ppermute x4 -> x8, starting transfers between devices: 3.26 us -> 18.7 us  [shifted(): lax.ppermute(block, axis, [(i, (i + distance) % count) for i in range(cou...]
    all_to_all x1, waiting for transfers between devices: 6.23 us -> 0.77 us  [on_device(): every_query = lax.all_to_all(turned, ('zc', 'y'), 0, 0, tiled=True)]
    ppermute x4, waiting for transfers between devices: 0.01 us -> 5.15 us  [shifted_x(): return lax.ppermute(block, ('xl', 'xh'), route)]
  transfers between devices with their start and end apart: 12 -> 16, of which waited for: 2 -> 4; matrix products, arithmetic and copies ran while one was open for 0% -> 0% of each run, Pallas kernels for 20% -> 20%
where the time goes in v3:
time: 91.5 us; the launch traced here: 91.1 us
  starting transfers between devices  36.4 us (40%)
  Pallas kernels  25.3 us (28%)
  blocking collectives  20.5 us (22%)
  waiting for transfers between devices  6.68 us (7%)
  local copies, waits for them, and re-layouts  1.95 us (2%)
    pallas_call x8, Pallas kernels, attend(): pl.pallas_call(functools.partial(attend_kernel, not carry, last, keep_blo...  18.9 us
    ppermute x8, starting transfers between devices, shifted(): lax.ppermute(block, axis, [(i, (i + distance) % count) for i in range(cou...  18.7 us
    all_to_all x1, blocking collectives, on_device(): parts = lax.all_to_all(partial, ('zc', 'y'), 0, 0, tiled=True)  11.9 us
    all_to_all x1, blocking collectives, on_device(): own = lax.all_to_all(flat, 'y', 0, 0, tiled=True).reshape(-1, 2 * WIDE)  8.66 us
    ppermute x2, starting transfers between devices, passed_along(): return lax.ppermute(block, axis, [(i - 1, i) for i in range(1, count)])  7.71 us
    ppermute x4, waiting for transfers between devices, shifted_x(): return lax.ppermute(block, ('xl', 'xh'), route)  5.15 us
    ppermute x1, starting transfers between devices, corner(): return lax.ppermute(block, AXES, route)  3.52 us
    pallas_call x2, Pallas kernels, pool_call(): pl.pallas_call(kernel, in_specs=[pl.BlockSpec(memory_space=pltpu.VMEM)] *...  3.46 us
  transfers between devices with their start and end apart: 16, of which 4 were waited for; matrix products, arithmetic and copies ran while one was open for 0% of the time, Pallas kernels for 20%

profile of v3, /device:TPU:1, one launch (start us, length us, event | category | flops | bytes accessed | tf_op | source)
XLA Modules:
  0.0 91.1 jit_solution(7801169749704160564)
XLA Ops:
  0.0 0.7 broadcast_in_dim.3.gain_ref
  0.7 1.1 %copy-done.2 = bf16[32,16,768]{2,1,0:T(8,128)(2,1)S(1)} copy-done((bf16[32,16,768]{2,1,0:T(8,128)(2,1)S(1)}, bf16[32,16,768]{2,1,0:T(8,128)(2,1)}, u32[]{:S(2)}) %copy-start.2) | copy-done | bytes 786456
  1.8 1.8 %shard_map.64 = (bf16[512,768]{1,0:T(8,128)(2,1)S(1)}, bf16[32,768]{1,0:T(8,128)(2,1)S(1)}, bf16[16,768]{1,0:T(8,128)(2,1)S(1)}, bf16[1,768]{1,0:T(2,128)(2,1)S(1)}) custom-call(bf16[32,16,768]{2,1,0:T(8,128)(2,1)S(1)} %copy-done.2, f32[1,768]{1,0:T(1,128)S(1)} %broadcast_in_dim.3.gain_ref), custom_call_target="tpu_custom_call" | custom-call | flops 4000000000 | bytes 1000000 | tf_op jit(solution)/shard_map/pallas_call | solution.py:91
  3.6 4.6 %collective-permute-start.1 = (bf16[32,768]{1,0:T(8,128)(2,1)S(1)}, bf16[32,768]{1,0:T(8,128)(2,1)S(1)}, u32[]{:S(2)}, u32[]{:S(2)}) collective-permute-start(bf16[32,768]{1,0:T(8,128)(2,1)S(1)} %get-tuple-element.35), channel_id=1, source_target_pairs={{0,1},{1,2},{2,3},{3,4},{4,5},{5,6},{6,7},{7,8},{8,9},{9,10},{10,1... | collective-permute-start | bytes 147464 | tf_op jit(solution)/shard_map/ppermute | solution.py:36
  8.2 3.1 %collective-permute-start = (bf16[16,768]{1,0:T(8,128)(2,1)S(1)}, bf16[16,768]{1,0:T(8,128)(2,1)S(1)}, u32[]{:S(2)}, u32[]{:S(2)}) collective-permute-start(bf16[16,768]{1,0:T(8,128)(2,1)S(1)} %get-tuple-element.34), channel_id=1, source_target_pairs={{0,16},{16,32},{32,48},{48,64},{64,80},{80,96},{96,112},{112,128},... | collective-permute-start | bytes 73736 | tf_op jit(solution)/shard_map/ppermute | solution.py:36
  11.3 3.5 %collective-permute-start.2 = (bf16[1,768]{1,0:T(2,128)(2,1)S(1)}, bf16[1,768]{1,0:T(2,128)(2,1)S(1)}, u32[]{:S(2)}, u32[]{:S(2)}) collective-permute-start(bf16[1,768]{1,0:T(2,128)(2,1)S(1)} %get-tuple-element.36), channel_id=1, source_target_pairs={{0,17},{1,18},{2,19},{3,20},{4,21},{5,22},{6,23},{7,24},{8,25},{9,... | collective-permute-start | bytes 4616 | tf_op jit(solution)/shard_map/ppermute | solution.py:42
  14.9 0.7 collective-permute-done.2.corner_ref
  15.6 1.5 %shard_map.65 = bf16[4,32,384]{2,1,0:T(8,128)(2,1)S(1)} custom-call(bf16[512,768]{1,0:T(8,128)(2,1)S(1)} %get-tuple-element.37.tokens_ref, bf16[16,768]{1,0:T(8,128)(2,1)S(1)} %collective-permute-done.upper_ref, bf16[32,768]{1,0:T(8,128)(2,1)S(1)} %collective-permute-done.1.left_ref, bf16[1,768]{1,0:T(2,128)(2,1)S(1)} %collective-permute-done.2.corner_ref, ...), custom_call_target="tpu_custom_call" | custom-call | flops 1500000000 | bytes 4000000 | tf_op jit(solution)/shard_map/pallas_call | solution.py:168
  17.1 8.7 %all_to_all.15 = bf16[4,32,384]{2,1,0:T(8,128)(2,1)S(1)} all-to-all(bf16[4,32,384]{2,1,0:T(8,128)(2,1)S(1)} %shard_map.65), channel_id=1, replica_groups=mesh['zq'=4,'zc'=2,'xl'=2,'xh'=2,'y'=4,'core'=2] {'y'}, dimensions={0} | all-to-all | bytes 196608 | tf_op jit(solution)/shard_map/all_to_all | solution.py:320
  25.8 7.6 %collective-permute-start.5 = (bf16[128,384]{1,0:T(8,128)(2,1)S(1)}, bf16[128,384]{1,0:T(8,128)(2,1)S(1)}, u32[]{:S(2)}, u32[]{:S(2)}) collective-permute-start(bf16[128,384]{1,0:T(8,128)(2,1)S(1)} %bitcast.1), channel_id=1, source_target_pairs={{0,192},{64,0},{128,64},{192,128},{1,193},{65,1},{129,65},{193,129... | collective-permute-start | bytes 294920 | tf_op jit(solution)/shard_map/ppermute | solution.py:25
  33.4 4.5 %collective-permute-start.3 = (bf16[128,384]{1,0:T(8,128)(2,1)S(1)}, bf16[128,384]{1,0:T(8,128)(2,1)S(1)}, u32[]{:S(2)}, u32[]{:S(2)}) collective-permute-start(bf16[128,384]{1,0:T(8,128)(2,1)S(1)} %bitcast.3), channel_id=1, source_target_pairs={{0,128},{64,192},{128,0},{192,64},{1,129},{65,193},{129,1},{193,65... | collective-permute-start | bytes 294920 | tf_op jit(solution)/shard_map/ppermute | solution.py:25
  37.8 2.0 %shard_map.66 = bf16[8,192,128]{2,1,0:T(8,128)(2,1)} custom-call(bf16[512,768]{1,0:T(8,128)(2,1)S(1)} %get-tuple-element.37.tokens_ref, bf16[16,768]{1,0:T(8,128)(2,1)S(1)} %collective-permute-done.upper_ref, bf16[32,768]{1,0:T(8,128)(2,1)S(1)} %collective-permute-done.1.left_ref, bf16[1,768]{1,0:T(2,128)(2,1)S(1)} %collective-permute-done.2.corner_ref, ...), custom_call_target="tpu_custom_call" | custom-call | flops 1500000000 | bytes 4000000 | tf_op jit(solution)/shard_map/pallas_call | solution.py:168
  39.8 3.5 %all-to-all-start.1 = ((bf16[8,192,128]{2,1,0:T(8,128)(2,1)}), bf16[8,192,128]{2,1,0:T(8,128)(2,1)S(1)}, u32[]{:S(2)}, u32[]{:S(2)}) async-start(bf16[8,192,128]{2,1,0:T(8,128)(2,1)} %shard_map.66), calls=%async_computation.1 | async-start | bytes 786432 | tf_op jit(solution)/shard_map/all_to_all | solution.py:325
  43.4 4.2 %collective-permute-start.8 = (bf16[512,384]{1,0:T(8,128)(2,1)S(1)}, bf16[512,384]{1,0:T(8,128)(2,1)S(1)}, u32[]{:S(2)}, u32[]{:S(2)}) collective-permute-start(bf16[512,384]{1,0:T(8,128)(2,1)S(1)} %constant_dynamic-update-slice_fusion.refs_0_), channel_id=1, source_target_pairs={{0,1},{1,0},{2,3},{3,2},{4,5},{5,4},{6,7},{7,6},{8,9},{9,8},{10,11... | collective-permute-start | bytes 1179656 | tf_op jit(solution)/shard_map/ppermute | solution.py:25
  47.5 1.5 %collective-permute-start.6 = (bf16[512,384]{1,0:T(8,128)(2,1)S(1)}, bf16[512,384]{1,0:T(8,128)(2,1)S(1)}, u32[]{:S(2)}, u32[]{:S(2)}) collective-permute-start(bf16[512,384]{1,0:T(8,128)(2,1)S(1)} %constant_dynamic-update-slice_fusion.refs_0_), channel_id=1, source_target_pairs={{0,16},{16,8},{8,24},{24,0},{1,17},{17,9},{9,25},{25,1},{2,18},{18... | collective-permute-start | bytes 1179656 | tf_op jit(solution)/shard_map/ppermute | solution.py:31
  49.0 0.8 all-to-all-done.1.q_ref
  49.8 2.1 %shard_map.67 = (f32[16,1024]{1,0:T(8,128)S(1)}, f32[192,1024]{1,0:T(8,128)S(1)}) custom-call(bf16[8,192,128]{2,1,0:T(8,128)(2,1)S(1)} %all-to-all-done.1.q_ref, bf16[512,384]{1,0:T(8,128)(2,1)S(1)} %constant_dynamic-update-slice_fusion.refs_0_), custom_call_target="tpu_custom_call" | custom-call | flops 1572864 | bytes 1024 | tf_op jit(solution)/shard_map/pallas_call | solution.py:266
  52.0 2.4 %shard_map.68 = (f32[16,1024]{1,0:T(8,128)S(1)}, f32[192,1024]{1,0:T(8,128)S(1)}) custom-call(bf16[8,192,128]{2,1,0:T(8,128)(2,1)S(1)} %all-to-all-done.1.q_ref, bf16[512,384]{1,0:T(8,128)(2,1)S(1)} %collective-permute-done.8.refs_0_, f32[16,1024]{1,0:T(8,128)S(1)} %get-tuple-element.39.refs_1_, ...), custom_call_target="tpu_custom_call", output_to_operand_aliasing={{0}: (2, {}), {1}: (3, {})} | custom-call | flops 1572864 | bytes 1024 | tf_op jit(solution)/shard_map/pallas_call | solution.py:266
  54.4 3.9 %collective-permute-done.7.refs_0_ = bf16[512,384]{1,0:T(8,128)(2,1)S(1)} collective-permute-done((bf16[512,384]{1,0:T(8,128)(2,1)S(1)}, bf16[512,384]{1,0:T(8,128)(2,1)S(1)}, u32[]{:S(2)}, u32[]{:S(2)}) %collective-permute-start.7) | collective-permute-done | bytes 393248 | tf_op jit(solution)/shard_map/ppermute | solution.py:31
  58.2 1.3 %collective-permute-done.6.refs_0_ = bf16[512,384]{1,0:T(8,128)(2,1)S(1)} collective-permute-done((bf16[512,384]{1,0:T(8,128)(2,1)S(1)}, bf16[512,384]{1,0:T(8,128)(2,1)S(1)}, u32[]{:S(2)}, u32[]{:S(2)}) %collective-permute-start.6) | collective-permute-done | bytes 393248 | tf_op jit(solution)/shard_map/ppermute | solution.py:31
  59.5 1.0 %collective-permute-start.12 = (bf16[512,384]{1,0:T(8,128)(2,1)S(1)}, bf16[512,384]{1,0:T(8,128)(2,1)S(1)}, u32[]{:S(2)}, u32[]{:S(2)}) collective-permute-start(bf16[512,384]{1,0:T(8,128)(2,1)S(1)} %collective-permute-done.6.refs_0_), channel_id=1, source_target_pairs={{0,1},{1,0},{2,3},{3,2},{4,5},{5,4},{6,7},{7,6},{8,9},{9,8},{10,11... | collective-permute-start | bytes 1179656 | tf_op jit(solution)/shard_map/ppermute | solution.py:25
  60.5 1.5 %collective-permute-start.10 = (bf16[256,384]{1,0:T(8,128)(2,1)S(1)}, bf16[256,384]{1,0:T(8,128)(2,1)S(1)}, u32[]{:S(2)}, u32[]{:S(2)}) collective-permute-start(bf16[256,384]{1,0:T(8,128)(2,1)S(1)} %slice.7), channel_id=1, source_target_pairs={{0,24},{16,0},{8,16},{24,8},{1,25},{17,1},{9,17},{25,9},{2,26},{18... | collective-permute-start | bytes 589832 | tf_op jit(solution)/shard_map/ppermute | solution.py:31
  62.1 2.4 %shard_map.69 = (f32[16,1024]{1,0:T(8,128)S(1)}, f32[192,1024]{1,0:T(8,128)S(1)}) custom-call(bf16[8,192,128]{2,1,0:T(8,128)(2,1)S(1)} %all-to-all-done.1.q_ref, bf16[512,384]{1,0:T(8,128)(2,1)S(1)} %collective-permute-done.6.refs_0_, f32[16,1024]{1,0:T(8,128)S(1)} %get-tuple-element.45.refs_1_, ...), custom_call_target="tpu_custom_call", output_to_operand_aliasing={{0}: (2, {}), {1}: (3, {})} | custom-call | flops 1572864 | bytes 1024 | tf_op jit(solution)/shard_map/pallas_call | solution.py:266
  64.5 2.4 %shard_map.70 = (f32[16,1024]{1,0:T(8,128)S(1)}, f32[192,1024]{1,0:T(8,128)S(1)}) custom-call(bf16[8,192,128]{2,1,0:T(8,128)(2,1)S(1)} %all-to-all-done.1.q_ref, bf16[512,384]{1,0:T(8,128)(2,1)S(1)} %collective-permute-done.12.refs_0_, f32[16,1024]{1,0:T(8,128)S(1)} %get-tuple-element.47.refs_1_, ...), custom_call_target="tpu_custom_call", output_to_operand_aliasing={{0}: (2, {}), {1}: (3, {})} | custom-call | flops 1572864 | bytes 1024 | tf_op jit(solution)/shard_map/pallas_call | solution.py:266
  66.9 2.4 %shard_map.71 = (f32[16,1024]{1,0:T(8,128)S(1)}, f32[192,1024]{1,0:T(8,128)S(1)}) custom-call(bf16[8,192,128]{2,1,0:T(8,128)(2,1)S(1)} %all-to-all-done.1.q_ref, bf16[512,384]{1,0:T(8,128)(2,1)S(1)} %collective-permute-done.7.refs_0_, f32[16,1024]{1,0:T(8,128)S(1)} %get-tuple-element.49.refs_1_, ...), custom_call_target="tpu_custom_call", output_to_operand_aliasing={{0}: (2, {}), {1}: (3, {})} | custom-call | flops 1572864 | bytes 1024 | tf_op jit(solution)/shard_map/pallas_call | solution.py:266
  69.3 2.4 %shard_map.72 = (f32[16,1024]{1,0:T(8,128)S(1)}, f32[192,1024]{1,0:T(8,128)S(1)}) custom-call(bf16[8,192,128]{2,1,0:T(8,128)(2,1)S(1)} %all-to-all-done.1.q_ref, bf16[512,384]{1,0:T(8,128)(2,1)S(1)} %collective-permute-done.11.refs_0_, f32[16,1024]{1,0:T(8,128)S(1)} %get-tuple-element.51.refs_1_, ...), custom_call_target="tpu_custom_call", output_to_operand_aliasing={{0}: (2, {}), {1}: (3, {})} | custom-call | flops 1572864 | bytes 1024 | tf_op jit(solution)/shard_map/pallas_call | solution.py:266
  71.7 1.1 %collective-permute-start.13 = (bf16[256,384]{1,0:T(8,128)(2,1)S(1)}, bf16[256,384]{1,0:T(8,128)(2,1)S(1)}, u32[]{:S(2)}, u32[]{:S(2)}) collective-permute-start(bf16[256,384]{1,0:T(8,128)(2,1)S(1)} %collective-permute-done.9.refs_0_), channel_id=1, source_target_pairs={{0,1},{1,0},{2,3},{3,2},{4,5},{5,4},{6,7},{7,6},{8,9},{9,8},{10,11... | collective-permute-start | bytes 589832 | tf_op jit(solution)/shard_map/ppermute | solution.py:25
  72.8 0.4 collective-permute-start.14
  73.2 2.4 %shard_map.73 = (f32[16,1024]{1,0:T(8,128)S(1)}, f32[192,1024]{1,0:T(8,128)S(1)}) custom-call(bf16[8,192,128]{2,1,0:T(8,128)(2,1)S(1)} %all-to-all-done.1.q_ref, bf16[256,384]{1,0:T(8,128)(2,1)S(1)} %collective-permute-done.9.refs_0_, bf16[256,384]{1,0:T(8,128)(2,1)S(1)} %collective-permute-done.10.refs_1_, ...), custom_call_target="tpu_custom_call", output_to_operand_aliasing={{0}: (3, {}), {1}: (4, {})} | custom-call | flops 1572864 | bytes 1024 | tf_op jit(solution)/shard_map/pallas_call | solution.py:266
  75.6 2.4 %shard_map.74 = bf16[8,208,128]{2,1,0:T(8,128)(2,1)S(1)} custom-call(bf16[8,192,128]{2,1,0:T(8,128)(2,1)S(1)} %all-to-all-done.1.q_ref, bf16[256,384]{1,0:T(8,128)(2,1)S(1)} %collective-permute-done.13.refs_0_, bf16[256,384]{1,0:T(8,128)(2,1)S(1)} %collective-permute-done.14.refs_1_, f32[16,1024]{1,0:T(8,128)S(1)} %get-tuple-element.59.refs_2_, ...), custom_call_target="tpu_custom_call" | custom-call | flops 1572864 | bytes 1024 | tf_op jit(solution)/shard_map/pallas_call | solution.py:266
  78.0 11.9 %all_to_all.16.parts_ref = bf16[8,208,128]{2,1,0:T(8,128)(2,1)S(1)} all-to-all(bf16[8,208,128]{2,1,0:T(8,128)(2,1)S(1)} %shard_map.74), channel_id=1, replica_groups=mesh['zq'=4,'zc'=2,'xl'=2,'xh'=2,'y'=4,'core'=2] {'zc','y'}, dimensions={0} | all-to-all | bytes 851968 | tf_op jit(solution)/shard_map/all_to_all | solution.py:340
  89.9 1.2 %shard_map.75 = bf16[16,8,768]{2,1,0:T(8,128)(2,1)} custom-call(bf16[8,208,128]{2,1,0:T(8,128)(2,1)S(1)} %all_to_all.16.parts_ref, bf16[768,768]{1,0:T(8,128)(2,1)S(1)} %copy-done), custom_call_target="tpu_custom_call" | custom-call | tf_op jit(solution)/shard_map/pallas_call | solution.py:306
  (31 shorter events, 0.2 us)
Async XLA Ops:
  0.7 1.1 %copy-start.2 = (bf16[32,16,768]{2,1,0:T(8,128)(2,1)S(1)}, bf16[32,16,768]{2,1,0:T(8,128)(2,1)}, u32[]{:S(2)}) copy-start(bf16[32,16,768]{2,1,0:T(8,128)(2,1)} %patches_ref.1) | copy-start | bytes 2359300
  1.8 13.8 %copy-start.1 = (bf16[768,2304]{1,0:T(8,128)(2,1)S(1)}, bf16[768,2304]{1,0:T(8,128)(2,1)}, u32[]{:S(2)}) copy-start(bf16[768,2304]{1,0:T(8,128)(2,1)} %w_ref.4) | copy-start | bytes 10616836
  1.8 13.8 %copy-start.3 = (f32[9,1536]{1,0:T(8,128)S(1)}, f32[9,1536]{1,0:T(8,128)}, u32[]{:S(2)}) copy-start(f32[9,1536]{1,0:T(8,128)} %pool_ref.2) | copy-start | bytes 165892
  3.6 34.2 %copy-start.4 = (f32[9,768]{1,0:T(8,128)S(1)}, f32[9,768]{1,0:T(8,128)}, u32[]{:S(2)}) copy-start(f32[9,768]{1,0:T(8,128)} %pool_ref.3) | copy-start | bytes 82948
  3.6 12.0 %collective-permute-start.1 = (bf16[32,768]{1,0:T(8,128)(2,1)S(1)}, bf16[32,768]{1,0:T(8,128)(2,1)S(1)}, u32[]{:S(2)}, u32[]{:S(2)}) collective-permute-start(bf16[32,768]{1,0:T(8,128)(2,1)S(1)} %get-tuple-element.35), channel_id=1, source_target_pairs={{0,1},{1,2},{2,3},{3,4},{4,5},{5,6},{6,7},{7,8},{8,9},{9,10},{10,1... | collective-permute-start | bytes 147464 | tf_op jit(solution)/shard_map/ppermute | solution.py:36
  8.2 7.4 %collective-permute-start = (bf16[16,768]{1,0:T(8,128)(2,1)S(1)}, bf16[16,768]{1,0:T(8,128)(2,1)S(1)}, u32[]{:S(2)}, u32[]{:S(2)}) collective-permute-start(bf16[16,768]{1,0:T(8,128)(2,1)S(1)} %get-tuple-element.34), channel_id=1, source_target_pairs={{0,16},{16,32},{32,48},{48,64},{64,80},{80,96},{96,112},{112,128},... | collective-permute-start | bytes 73736 | tf_op jit(solution)/shard_map/ppermute | solution.py:36
  11.3 4.3 %collective-permute-start.2 = (bf16[1,768]{1,0:T(2,128)(2,1)S(1)}, bf16[1,768]{1,0:T(2,128)(2,1)S(1)}, u32[]{:S(2)}, u32[]{:S(2)}) collective-permute-start(bf16[1,768]{1,0:T(2,128)(2,1)S(1)} %get-tuple-element.36), channel_id=1, source_target_pairs={{0,17},{1,18},{2,19},{3,20},{4,21},{5,22},{6,23},{7,24},{8,25},{9,... | collective-permute-start | bytes 4616 | tf_op jit(solution)/shard_map/ppermute | solution.py:42
  25.8 17.5 %collective-permute-start.5 = (bf16[128,384]{1,0:T(8,128)(2,1)S(1)}, bf16[128,384]{1,0:T(8,128)(2,1)S(1)}, u32[]{:S(2)}, u32[]{:S(2)}) collective-permute-start(bf16[128,384]{1,0:T(8,128)(2,1)S(1)} %bitcast.1), channel_id=1, source_target_pairs={{0,192},{64,0},{128,64},{192,128},{1,193},{65,1},{129,65},{193,129... | collective-permute-start | bytes 294920 | tf_op jit(solution)/shard_map/ppermute | solution.py:25
  33.4 9.9 %collective-permute-start.4 = (bf16[128,384]{1,0:T(8,128)(2,1)S(1)}, bf16[128,384]{1,0:T(8,128)(2,1)S(1)}, u32[]{:S(2)}, u32[]{:S(2)}) collective-permute-start(bf16[128,384]{1,0:T(8,128)(2,1)S(1)} %bitcast.2), channel_id=1, source_target_pairs={{0,64},{64,128},{128,192},{192,0},{1,65},{65,129},{129,193},{193,1... | collective-permute-start | bytes 294920 | tf_op jit(solution)/shard_map/ppermute | solution.py:25
  33.4 9.9 %collective-permute-start.3 = (bf16[128,384]{1,0:T(8,128)(2,1)S(1)}, bf16[128,384]{1,0:T(8,128)(2,1)S(1)}, u32[]{:S(2)}, u32[]{:S(2)}) collective-permute-start(bf16[128,384]{1,0:T(8,128)(2,1)S(1)} %bitcast.3), channel_id=1, source_target_pairs={{0,128},{64,192},{128,0},{192,64},{1,129},{65,193},{129,1},{193,65... | collective-permute-start | bytes 294920 | tf_op jit(solution)/shard_map/ppermute | solution.py:25
  39.8 10.0 %all-to-all-start.1 = ((bf16[8,192,128]{2,1,0:T(8,128)(2,1)}), bf16[8,192,128]{2,1,0:T(8,128)(2,1)S(1)}, u32[]{:S(2)}, u32[]{:S(2)}) async-start(bf16[8,192,128]{2,1,0:T(8,128)(2,1)} %shard_map.66), calls=%async_computation.1 | async-start | bytes 786432 | tf_op jit(solution)/shard_map/all_to_all | solution.py:325
  43.4 8.6 %collective-permute-start.8 = (bf16[512,384]{1,0:T(8,128)(2,1)S(1)}, bf16[512,384]{1,0:T(8,128)(2,1)S(1)}, u32[]{:S(2)}, u32[]{:S(2)}) collective-permute-start(bf16[512,384]{1,0:T(8,128)(2,1)S(1)} %constant_dynamic-update-slice_fusion.refs_0_), channel_id=1, source_target_pairs={{0,1},{1,0},{2,3},{3,2},{4,5},{5,4},{6,7},{7,6},{8,9},{9,8},{10,11... | collective-permute-start | bytes 1179656 | tf_op jit(solution)/shard_map/ppermute | solution.py:25
  47.5 10.7 %collective-permute-start.7 = (bf16[512,384]{1,0:T(8,128)(2,1)S(1)}, bf16[512,384]{1,0:T(8,128)(2,1)S(1)}, u32[]{:S(2)}, u32[]{:S(2)}) collective-permute-start(bf16[512,384]{1,0:T(8,128)(2,1)S(1)} %constant_dynamic-update-slice_fusion.refs_0_), channel_id=1, source_target_pairs={{0,24},{16,0},{8,16},{24,8},{1,25},{17,1},{9,17},{25,9},{2,26},{18... | collective-permute-start | bytes 1179656 | tf_op jit(solution)/shard_map/ppermute | solution.py:31
  47.5 12.0 %collective-permute-start.6 = (bf16[512,384]{1,0:T(8,128)(2,1)S(1)}, bf16[512,384]{1,0:T(8,128)(2,1)S(1)}, u32[]{:S(2)}, u32[]{:S(2)}) collective-permute-start(bf16[512,384]{1,0:T(8,128)(2,1)S(1)} %constant_dynamic-update-slice_fusion.refs_0_), channel_id=1, source_target_pairs={{0,16},{16,8},{8,24},{24,0},{1,17},{17,9},{9,25},{25,1},{2,18},{18... | collective-permute-start | bytes 1179656 | tf_op jit(solution)/shard_map/ppermute | solution.py:31
  59.5 5.0 %collective-permute-start.12 = (bf16[512,384]{1,0:T(8,128)(2,1)S(1)}, bf16[512,384]{1,0:T(8,128)(2,1)S(1)}, u32[]{:S(2)}, u32[]{:S(2)}) collective-permute-start(bf16[512,384]{1,0:T(8,128)(2,1)S(1)} %collective-permute-done.6.refs_0_), channel_id=1, source_target_pairs={{0,1},{1,0},{2,3},{3,2},{4,5},{5,4},{6,7},{7,6},{8,9},{9,8},{10,11... | collective-permute-start | bytes 1179656 | tf_op jit(solution)/shard_map/ppermute | solution.py:25
  60.5 8.8 %collective-permute-start.11 = (bf16[512,384]{1,0:T(8,128)(2,1)S(1)}, bf16[512,384]{1,0:T(8,128)(2,1)S(1)}, u32[]{:S(2)}, u32[]{:S(2)}) collective-permute-start(bf16[512,384]{1,0:T(8,128)(2,1)S(1)} %collective-permute-done.7.refs_0_), channel_id=1, source_target_pairs={{0,1},{1,0},{2,3},{3,2},{4,5},{5,4},{6,7},{7,6},{8,9},{9,8},{10,11... | collective-permute-start | bytes 1179656 | tf_op jit(solution)/shard_map/ppermute | solution.py:25
  60.5 11.1 %collective-permute-start.10 = (bf16[256,384]{1,0:T(8,128)(2,1)S(1)}, bf16[256,384]{1,0:T(8,128)(2,1)S(1)}, u32[]{:S(2)}, u32[]{:S(2)}) collective-permute-start(bf16[256,384]{1,0:T(8,128)(2,1)S(1)} %slice.7), channel_id=1, source_target_pairs={{0,24},{16,0},{8,16},{24,8},{1,25},{17,1},{9,17},{25,9},{2,26},{18... | collective-permute-start | bytes 589832 | tf_op jit(solution)/shard_map/ppermute | solution.py:31
  62.1 9.6 %collective-permute-start.9 = (bf16[256,384]{1,0:T(8,128)(2,1)S(1)}, bf16[256,384]{1,0:T(8,128)(2,1)S(1)}, u32[]{:S(2)}, u32[]{:S(2)}) collective-permute-start(bf16[256,384]{1,0:T(8,128)(2,1)S(1)} %slice.6), channel_id=1, source_target_pairs={{0,16},{16,8},{8,24},{24,0},{1,17},{17,9},{9,25},{25,1},{2,18},{18... | collective-permute-start | bytes 589832 | tf_op jit(solution)/shard_map/ppermute | solution.py:31
  66.9 23.0 %copy-start = (bf16[768,768]{1,0:T(8,128)(2,1)S(1)}, bf16[768,768]{1,0:T(8,128)(2,1)}, u32[]{:S(2)}) copy-start(bf16[768,768]{1,0:T(8,128)(2,1)} %w_ref.5) | copy-start | bytes 3538948
  71.7 3.9 %collective-permute-start.13 = (bf16[256,384]{1,0:T(8,128)(2,1)S(1)}, bf16[256,384]{1,0:T(8,128)(2,1)S(1)}, u32[]{:S(2)}, u32[]{:S(2)}) collective-permute-start(bf16[256,384]{1,0:T(8,128)(2,1)S(1)} %collective-permute-done.9.refs_0_), channel_id=1, source_target_pairs={{0,1},{1,0},{2,3},{3,2},{4,5},{5,4},{6,7},{7,6},{8,9},{9,8},{10,11... | collective-permute-start | bytes 589832 | tf_op jit(solution)/shard_map/ppermute | solution.py:25
  72.8 2.8 %collective-permute-start.14 = (bf16[256,384]{1,0:T(8,128)(2,1)S(1)}, bf16[256,384]{1,0:T(8,128)(2,1)S(1)}, u32[]{:S(2)}, u32[]{:S(2)}) collective-permute-start(bf16[256,384]{1,0:T(8,128)(2,1)S(1)} %collective-permute-done.10.refs_1_), channel_id=1, source_target_pairs={{0,1},{1,0},{2,3},{3,2},{4,5},{5,4},{6,7},{7,6},{8,9},{9,8},{10,11... | collective-permute-start | bytes 589832 | tf_op jit(solution)/shard_map/ppermute | solution.py:25
